TPU v7x, 32 devices: a whole 2x2x4 slice. The times are simulated.
32 devices in a mesh: batch: 16 (over z, x, core), query: 2 (over y).
Axes of the slice: x: 2, y: 2, z: 4, core: 2. Of those that a mesh axis runs over, the one named last changes fastest.
Arguments:
- latents: bfloat16 [96, 100, 768], P('batch', 'query'), may hold values from -6 to 6
- queries: bfloat16 [96, 96, 768], P('batch', 'query'), may hold values from -6 to 6
- order: int32 [96, 196], P('batch'), may hold values from 0 to 195, each once within a row
- weight_query: bfloat16 [768, 768], P(('batch', 'query')), may hold values from -0.21875 to 0.21875
- bias_query: bfloat16 [768], P(('batch', 'query')), may hold values from -4 to 4
- weight_key: bfloat16 [768, 768], P(('batch', 'query')), may hold values from -0.21875 to 0.21875
- weight_value: bfloat16 [768, 768], P(('batch', 'query')), may hold values from -0.21875 to 0.21875
- bias_value: bfloat16 [768], P(('batch', 'query')), may hold values from -0.75 to 0.75
- weight_out: bfloat16 [768, 768], P(('batch', 'query')), may hold values from -1.75 to 1.75
- bias_out: bfloat16 [768], P(('batch', 'query')), may hold values from -4 to 4
- gain_query: bfloat16 [768], P(('batch', 'query')), may hold values from 0.099609375 to 1.8984375
- shift_query: bfloat16 [768], P(('batch', 'query')), may hold values from -4 to 4
- gain_key: bfloat16 [768], P(('batch', 'query')), may hold values from 0.099609375 to 1.8984375
- gain_value: bfloat16 [768], P(('batch', 'query')), may hold values from 0.099609375 to 1.8984375
- shift_value: bfloat16 [768], P(('batch', 'query')), may hold values from -1.5 to 1.5
- scale_attention: bfloat16 [768], P(('batch', 'query')), may hold values from 0.5 to 2
- weight_up: bfloat16 [768, 3072], P(('batch', 'query')), may hold values from -0.21875 to 0.21875
- bias_up: bfloat16 [3072], P(('batch', 'query')), may hold values from -4 to 4
- weight_down: bfloat16 [3072, 768], P(('batch', 'query')), may hold values from -0.109375 to 0.109375
- bias_down: bfloat16 [768], P(('batch', 'query')), may hold values from -4 to 4
- gain_feed: bfloat16 [768], P(('batch', 'query')), may hold values from 0.099609375 to 1.8984375
- shift_feed: bfloat16 [768], P(('batch', 'query')), may hold values from -4 to 4
- scale_feed: bfloat16 [768], P(('batch', 'query')), may hold values from 0.5 to 2
- cotangent: bfloat16 [96, 96, 768], P('batch', 'query'), may hold values from -6 to 6
Outputs:
- mixed: bfloat16 [96, 96, 768], P('batch', 'query')
- latents_gradient: float32 [96, 100, 768], P('batch', 'query')
- queries_gradient: float32 [96, 96, 768], P('batch', 'query')
- weight_query_gradient: float32 [768, 768], P(('batch', 'query'))
- bias_query_gradient: float32 [768], P(('batch', 'query'))
- weight_key_gradient: float32 [768, 768], P(('batch', 'query'))
- weight_value_gradient: float32 [768, 768], P(('batch', 'query'))
- bias_value_gradient: float32 [768], P(('batch', 'query'))
- weight_out_gradient: float32 [768, 768], P(('batch', 'query'))
- bias_out_gradient: float32 [768], P(('batch', 'query'))
- gain_query_gradient: float32 [768], P(('batch', 'query'))
- shift_query_gradient: float32 [768], P(('batch', 'query'))
- gain_key_gradient: float32 [768], P(('batch', 'query'))
- gain_value_gradient: float32 [768], P(('batch', 'query'))
- shift_value_gradient: float32 [768], P(('batch', 'query'))
- scale_attention_gradient: float32 [768], P(('batch', 'query'))
- weight_up_gradient: float32 [768, 3072], P(('batch', 'query'))
- bias_up_gradient: float32 [3072], P(('batch', 'query'))
- weight_down_gradient: float32 [3072, 768], P(('batch', 'query'))
- bias_down_gradient: float32 [768], P(('batch', 'query'))
- gain_feed_gradient: float32 [768], P(('batch', 'query'))
- shift_feed_gradient: float32 [768], P(('batch', 'query'))
- scale_feed_gradient: float32 [768], P(('batch', 'query'))
Inputs may be any that keep to these rules, and one draw needn't show every extreme that they name: Each row names every patch of its crop once: the first 100 entries belong to the latents' rows in order, the others to the queries' rows in order.
All inputs are finite; a program needn't handle non-finite values.
Results may differ from a plain program's by a relative error of at most 0.015.
Values may be sent and summed in bfloat16 or wider, within the bound.
No kernel may reach another device: no remote copies, remote signals or barrier semaphores. Data moves between devices by JAX's collectives and lax.ppermute only.
A program may use at most 192 MiB of HBM per device.

v0:
```python
import functools
import math

import jax
import jax.numpy as jnp
import ml_dtypes
import numpy as np
from jax import lax
from jax.experimental import pallas as pl
from jax.experimental.pallas import tpu as pltpu
from jax.sharding import Mesh
from jax.sharding import PartitionSpec as P

BATCH = ("ring", "x", "core")
HEADS = 12
GRID = 14
GROUP = 4
CHUNK = 768
EPSILON = 1e-06
BIAS_QUERY = 0
BIAS_VALUE = 1
BIAS_OUT = 2
GAIN_QUERY = 3
SHIFT_QUERY = 4
GAIN_KEY = 5
GAIN_VALUE = 6
SHIFT_VALUE = 7
SCALE_ATTENTION = 8
BIAS_DOWN = 9
GAIN_FEED = 10
SHIFT_FEED = 11
SCALE_FEED = 12
SMALLS = 13
BIAS_ROW = 16
LINE_ROWS = 24
ANY = pl.ANY
SMEM = pltpu.SMEM


class Net:
    def __init__(self):
        self.ring = lax.axis_size("ring")
        batch = 4 * self.ring
        self.units = batch
        self.count = batch * lax.axis_size("query")
        self.at_ring, self.at_x, self.at_core = lax.axis_index("ring"), lax.axis_index("x"), lax.axis_index("core")
        self.at_y = lax.axis_index("query")
        slot = jnp.arange(batch)
        core, x, step = slot // (2 * self.ring), (slot // self.ring) % 2, slot % self.ring
        rest = 2 * (x ^ self.at_x) + (core ^ self.at_core)
        self.gathered = (4 * ((self.at_ring - step) % self.ring) + rest).astype(jnp.int32)
        self.scattered = (4 * ((self.at_ring + step) % self.ring) + rest).astype(jnp.int32)

    def turn(self, values, step):
        return lax.ppermute(values, "ring", [(place, (place + step) % self.ring) for place in range(self.ring)])

    def turns(self, values):
        return [values] + [self.turn(values, step) for step in range(1, self.ring)]

    def swap_x(self, values):
        return lax.ppermute(values, "x", [(0, 1), (1, 0)])

    def swap_core(self, values):
        return lax.ppermute(values, "core", [(0, 1), (1, 0)])

    def swap_y(self, values):
        return lax.ppermute(values, "query", [(0, 1), (1, 0)])

    def pair(self, own, came, tiles):
        first = jnp.where(self.at_y == 0, own, came)
        last = jnp.where(self.at_y == 0, came, own)
        slots, rows, width = own.shape
        both = jnp.stack([part.reshape(slots, tiles, -1, width) for part in (first, last)], axis=2)
        return both.reshape(slots, tiles, -1, width)

    def core_pairs(self, parts):
        return list(parts) + [self.swap_core(part) for part in parts]

    def aligned(self, parts, units):
        places = self.gathered[:units] if units == self.units else self.gathered[:units] // 2
        if parts[0].shape[2] % 16 == 0:
            return parts, places
        _, tiles, _, width = parts[0].shape
        back = jnp.zeros_like(places).at[places].set(jnp.arange(units, dtype=jnp.int32))
        whole = jnp.swapaxes(jnp.concatenate(parts)[back], 0, 1)
        count = whole.shape[1] * whole.shape[2] // 48
        return [jnp.swapaxes(whole.reshape(tiles, count, 48, width), 0, 1)], jnp.arange(count, dtype=jnp.int32)

    def aligned_cores(self, parts):
        if parts[0].shape[2] % 16 == 0:
            return parts, self.gathered
        flat = jnp.concatenate([part[:, core] for core in range(2) for part in parts])[:, None]
        return self.aligned([flat], self.units)

    def feed_units(self, following, units):
        down, down_y, up, up_x = following
        down_parts, down_places = self.aligned([self.pair(down, down_y, 1)], units)
        up_parts, up_places = self.aligned_cores([up, up_x])
        down_plan = [(0, (index, 0)) for index in range(down_parts[0].shape[0])]
        up_plan = [
            (1 + part, (index, tile))
            for tile in range(up_parts[0].shape[1]) for part, array in enumerate(up_parts) for index in range(array.shape[0])
        ]
        return [*down_parts, *up_parts], (down_plan, down_places, up_plan, up_places)

    def slots(self, rows):
        if rows // self.units % 16 == 0:
            return self.units, self.scattered
        return rows // 48, jnp.arange(rows // 48, dtype=jnp.int32)

    def unaligned(self, keep, send):
        tiles, _, _, width = keep.shape
        if keep.shape[1] * 2 != self.units or keep.shape[2] % 16 != 0:
            whole = jnp.concatenate([keep, send], axis=1).reshape(tiles, self.units, -1, width)[:, self.scattered]
            keep, send = whole[:, : self.units // 2], whole[:, self.units // 2 :]
        return [part.reshape(tiles, self.units // 2, 2, -1, width) for part in (keep, send)]

    def mine(self, part):
        return lax.dynamic_index_in_dim(part, self.at_y, 2, keepdims=False).astype(jnp.float32)

    def other(self, part):
        return lax.dynamic_index_in_dim(part, 1 - self.at_y, 2, keepdims=False).astype(jnp.float32)

    def moves(self, sends, *others):
        kinds = dict(x=self.swap_x, y=self.swap_y, core=self.swap_core, turn=self.turn)
        values, others = lax.optimization_barrier(([send[1] for send in sends], others))
        came = [kinds[kind](value, *rest) for (kind, _, *rest), value in zip(sends, values)]
        return came, others

    def scatter_second(self, first):
        keep_a, keep_b, came_a, came_b = first
        ring, f32, low = self.ring, jnp.float32, jnp.bfloat16
        away_a = (keep_a[:, ring:].astype(f32) + came_a[:, ring:].astype(f32)).astype(low)
        away_b = (self.other(keep_b) + self.other(came_b)).astype(low)
        return ((keep_a[:, :ring], came_a[:, :ring]), (keep_b, came_b)), [("x", away_a), ("y", away_b)]

    def feed_second(self, keep, send, up):
        return ((keep,), (up,)), [("x", send), ("y", self.other(up).astype(up.dtype))]

    def scatter_third(self, kept, came):
        (parts_a, parts_b), (next_a, next_b) = kept, came
        ring, f32, low = self.ring, jnp.float32, jnp.bfloat16
        total = lambda pick, parts: sum((pick(part) for part in parts[1:]), pick(parts[0]))
        parts_a = (*parts_a, next_a)
        away_a = total(self.other, parts_a).astype(low)
        away_b = total(lambda part: self.mine(part[:, ring:]), parts_b) + next_b[:, ring:].astype(f32)
        return (parts_a, (parts_b, next_b)), [("y", away_a), ("x", away_b.astype(low))]

    def scatter_fourth(self, kept, came):
        (parts_a, (parts_b, next_b)), (last_a, last_b) = kept, came
        ring, f32, low = self.ring, jnp.float32, jnp.bfloat16
        total = lambda pick, parts: sum((pick(part) for part in parts[1:]), pick(parts[0]))
        sum_a = total(self.mine, parts_a) + last_a.astype(f32)
        sum_b = total(lambda part: self.mine(part[:, :ring]), parts_b) + next_b[:, :ring].astype(f32) + last_b.astype(f32)
        flat = lambda part: part.reshape(-1, part.shape[-1])
        pieces = [jnp.concatenate([flat(sum_a[:, step]), flat(sum_b[:, step])]) for step in range(self.ring)]
        shape = (sum_a.shape[0],) + sum_a.shape[2:]
        return (shape, pieces[0]), [("turn", pieces[step].astype(low), step) for step in range(1, self.ring)]

    def scatter_last(self, kept, came):
        shape, total = kept
        for piece in came:
            total = total + piece.astype(jnp.float32)
        rows = shape[0] * shape[1]
        return total[:rows].reshape(shape), total[rows:]


def standard(values):
    centered = values - jnp.mean(values, axis=-1, keepdims=True)
    scale = lax.rsqrt(jnp.mean(centered * centered, axis=-1, keepdims=True) + EPSILON)
    return centered * scale, scale


def standard_back(grad, normed, scale, gain):
    slope = grad * gain
    inner = jnp.mean(slope * normed, axis=-1, keepdims=True)
    return (slope - jnp.mean(slope, axis=-1, keepdims=True) - normed * inner) * scale


def wide(ref):
    return ref[...].astype(jnp.float32)


def dot(left, right, left_dim=1, right_dim=0):
    return lax.dot_general(left, right, (((left_dim,), (right_dim,)), ((), ())), preferred_element_type=jnp.float32)


def rows_sum(values):
    return jnp.sum(values, axis=0, keepdims=True)


def by_head(rows):
    lane = lax.broadcasted_iota(jnp.int32, rows.shape, 1)
    head = rows.shape[1] // GROUP
    zero = jnp.zeros_like(rows)
    return jnp.concatenate(
        [jnp.where((lane >= head * h) & (lane < head * (h + 1)), rows, zero) for h in range(GROUP)], axis=0
    )


def from_heads(stacked):
    count = stacked.shape[0] // GROUP
    head = stacked.shape[1] // GROUP
    lane = lax.broadcasted_iota(jnp.int32, (count, stacked.shape[1]), 1)
    result = stacked[:count]
    for h in range(1, GROUP):
        result = jnp.where(lane >= head * h, stacked[count * h : count * (h + 1)], result)
    return result


def fetch(slots_ref, units, whole, sem):
    for slot, unit in enumerate(units):
        rows = unit.shape[0]
        place = pl.multiple_of(slots_ref[slot] * rows, 16)
        pltpu.make_async_copy(unit, whole.at[pl.ds(place, rows)], sem).start()


def units_of(parts, tile):
    return [part.at[index, tile] for part in parts for index in range(part.shape[0])]


def store(slots_ref, whole, parts, sem):
    slot = 0
    for part in parts:
        rows = part.shape[-2]
        for index in range(part.shape[-3]):
            if len(part.shape) == 3:
                place = pl.multiple_of(slots_ref[slot] * rows, 16)
                pltpu.make_async_copy(whole.at[pl.ds(place, rows)], part.at[index], sem).start()
            else:
                for half in range(2):
                    place = pl.multiple_of((2 * slots_ref[slot] + half) * rows, 16)
                    pltpu.make_async_copy(whole.at[pl.ds(place, rows)], part.at[half, index], sem).start()
            slot += 1


def finish(whole, sem):
    pltpu.make_async_copy(whole, whole, sem).wait()


def layout(visible, masked):
    padded = -(-visible // 8) * 8
    starts = (0, masked, 2 * masked, 2 * masked + padded)
    return starts, -(-(2 * masked + 2 * padded) // 16) * 16


def prepare_kernel(
    place_ref, own_ref, own_latent_ref, came_ref, table_ref, key_ref, value_ref, key_scale_ref, value_scale_ref, rows_ref
):
    masked, visible = own_ref.shape[1], own_latent_ref.shape[1]
    starts, _ = layout(visible, masked)
    rows_ref[...] = jnp.zeros_like(rows_ref)
    rows_ref[:masked] = wide(own_ref.at[0])
    rows_ref[masked : 2 * masked] = came_ref[0, :masked].astype(jnp.float32)
    rows_ref[starts[2] : starts[2] + visible] = wide(own_latent_ref.at[0])
    rows_ref[starts[3] : starts[3] + visible] = came_ref[0, 2 * masked :].astype(jnp.float32)
    rows = rows_ref[...]
    place = place_ref[0]
    lane = lax.broadcasted_iota(jnp.int32, (rows.shape[0], table_ref.shape[0]), 1)
    wanted = jnp.where((lane & 16) == 0, place[:, 0:1], place[:, 1:2])
    chosen = jnp.where((lane & 15) == wanted, 1.0, 0.0).astype(jnp.bfloat16)
    position = dot(chosen, table_ref[...])
    key_ref[0], key_scale_ref[0] = standard(rows + position)
    value_ref[0], value_scale_ref[0] = standard(rows)


def attend_kernel(visible, factor, parts_a, parts_b, *refs):
    slots_ref, key_hat_ref, value_hat_ref, own_ref, came_ref, small_ref = refs[:6]
    part_a, part_b, refs = refs[6 : 6 + parts_a], refs[6 + parts_a : 6 + parts_a + parts_b], refs[6 + parts_a + parts_b :]
    query_ref, key_ref, value_ref, probs_ref, attended_ref, branch_ref, feed_hat_ref, feed_scale_ref, feed_ref = refs[-17:-8]
    normed_refs = refs[-8:-5]
    query_w, key_w, value_w, out_w, sems = refs[-5:]

    @pl.when(pl.program_id(0) == 0)
    def _():
        for index, (parts, tile, whole) in enumerate(
            ((part_a, 0, query_w), (part_a, 1, key_w), (part_b, 0, value_w), (part_b, 1, out_w))
        ):
            fetch(slots_ref, units_of(parts, tile), whole, sems.at[index])
        for index, whole in enumerate((query_w, key_w, value_w, out_w)):
            finish(whole, sems.at[index])

    small = lambda row: small_ref[row : row + 1]
    count = attended_ref.shape[1]
    low = jnp.bfloat16
    query_normed = (key_hat_ref[0, :count] * small(GAIN_QUERY) + small(SHIFT_QUERY)).astype(low)
    key_normed = (key_hat_ref[0] * small(GAIN_KEY)).astype(low)
    value_normed = (value_hat_ref[0] * small(GAIN_VALUE) + small(SHIFT_VALUE)).astype(low)
    for ref, value in zip(normed_refs, (query_normed, key_normed, value_normed)):
        ref[0] = value
    query_ref[0] = (dot(query_normed, query_w[...]) + small(BIAS_QUERY)).astype(low)
    key_ref[0] = dot(key_normed, key_w[...]).astype(low)
    value_ref[0] = (dot(value_normed, value_w[...]) + small(BIAS_VALUE)).astype(low)
    width = key_ref.shape[2] // probs_ref.shape[1]
    for quad in range(probs_ref.shape[1]):
        lanes = slice(width * quad, width * (quad + 1))
        scores = dot(key_ref[0, :, lanes], by_head(query_ref[0, :, lanes]), 1, 1) * factor
        row = lax.broadcasted_iota(jnp.int32, scores.shape, 0)
        starts, _ = layout(visible, own_ref.shape[1])
        real = (row < starts[2] + visible) | ((row >= starts[3]) & (row < starts[3] + visible))
        scores = jnp.where(real, scores, -1e30)
        raised = jnp.exp(scores - jnp.max(scores, axis=0, keepdims=True))
        probs = (raised * (1.0 / rows_sum(raised))).astype(low)
        probs_ref[0, quad] = probs
        attended_ref[0, :, lanes] = from_heads(dot(probs, value_ref[0, :, lanes], 0, 0)).astype(low)
    branch = dot(attended_ref[0], out_w[...]) + small(BIAS_OUT)
    branch_ref[0] = branch
    queries = jnp.concatenate([wide(own_ref.at[0]), wide(came_ref.at[0])], axis=0)
    hat, scale = standard(queries + small(SCALE_ATTENTION) * branch)
    feed_hat_ref[0] = hat
    feed_scale_ref[0] = scale
    feed_ref[0] = (hat * small(GAIN_FEED) + small(SHIFT_FEED)).astype(low)


def feed_kernel(last, down_plan, up_plan, parts, *refs):
    slots_ref, down_slots_ref, out_slots_ref, down_out_slots_ref, core_ref = refs[:5]
    feed_ref, feed_other_ref, cot_refs, small_ref, refs = refs[5], refs[6], refs[7:11], refs[11], refs[12:]
    part_refs = refs[:parts]
    down_w, up_w, down_grad, up_grad, sems = refs[-5:]
    refs = refs[parts:-5]
    outs, refs = refs[:3], refs[3:]
    low = jnp.bfloat16
    small = lambda row: small_ref[row : row + 1]
    fetch(slots_ref, [part_refs[part].at[where] for part, where in up_plan], up_w, sems.at[0])
    fetch(down_slots_ref, [part_refs[part].at[where] for part, where in down_plan], down_w, sems.at[1])
    cotangent = []
    for first, second in (cot_refs[:2], cot_refs[2:]):
        for crop in range(first.shape[0]):
            cotangent += [wide(first.at[crop]), wide(second.at[crop])]
    low_grad = (small(SCALE_FEED) * jnp.concatenate(cotangent, axis=0)).astype(low)
    feed = jnp.concatenate([feed_ref[...], feed_other_ref[...]], axis=0)
    bias = small_ref[pl.ds(BIAS_ROW + 2 * last + core_ref[0], 1)]
    finish(up_w, sems.at[0])
    raised = dot(feed, up_w[...]) + bias
    share = 0.5 * (1.0 + lax.erf(raised * (0.5**0.5)))
    activated = (raised * share).astype(low)
    slope = share + raised * jnp.exp(-0.5 * raised * raised) * ((2.0 * math.pi) ** -0.5)
    down_grad[...] = dot(activated, low_grad, 0, 0).astype(low)
    keep, send, up_out = outs
    store(down_out_slots_ref, down_grad, [keep.at[0], send.at[0]], sems.at[2])
    finish(down_w, sems.at[1])
    raised_grad = (dot(low_grad, down_w[...], 1, 1) * slope).astype(low)
    up_grad[...] = dot(feed, raised_grad, 0, 0).astype(low)
    store(out_slots_ref, up_grad, [up_out.at[tile] for tile in range(up_out.shape[0])], sems.at[3])
    refs[0][...] = rows_sum(raised_grad.astype(jnp.float32))
    lowered = dot(activated, down_w[...])
    grad = dot(raised_grad, up_w[...], 1, 1)
    rows = feed_ref.shape[0]
    for index, value in enumerate((lowered, grad)):
        refs[1 + index][...] = value[:rows]
        if last:
            refs[3 + index][...] = value[rows:].astype(low)
        else:
            refs[3][rows * index : rows * (index + 1)] = value[rows:].astype(low)
    finish(down_grad, sems.at[2])
    finish(up_grad, sems.at[3])


def attend_back_kernel(factor, parts_b, *refs):
    slots_ref, query_ref, key_ref, value_ref, probs_ref = refs[:5]
    lowered_refs, back_refs = refs[5:9], refs[9:13]
    cot_own_ref, cot_came_ref, own_ref, came_ref, branch_ref, hat_ref, scale_ref, small_ref = refs[13:21]
    part_b = refs[21 : 21 + parts_b]
    mixed_own_ref, mixed_came_ref, middle_grad_ref, branch_grad_ref, sums_ref = refs[-10:-5]
    query_grad, key_grad, value_grad, out_w, sem = refs[-5:]
    small = lambda row: small_ref[row : row + 1]
    low = jnp.bfloat16

    @pl.when(pl.program_id(0) == 0)
    def _():
        fetch(slots_ref, units_of(part_b, 1), out_w, sem)
        sums_ref[...] = jnp.zeros_like(sums_ref)

    join = lambda first, second: jnp.concatenate([wide(first.at[0]), wide(second.at[0])], axis=0)
    cotangent = join(cot_own_ref, cot_came_ref)
    lowered = sum((wide(ref.at[0]) for ref in lowered_refs), small(BIAS_DOWN))
    branch = branch_ref[0]
    middle = join(own_ref, came_ref) + small(SCALE_ATTENTION) * branch
    mixed = (middle + small(SCALE_FEED) * lowered).astype(low)
    half = mixed_own_ref.shape[1]
    mixed_own_ref[0] = mixed[:half]
    mixed_came_ref[0] = mixed[half:]
    grad = sum((wide(ref.at[0]) for ref in back_refs[1:]), wide(back_refs[0].at[0]))
    hat = hat_ref[0]
    middle_grad = cotangent + standard_back(grad, hat, scale_ref[0], small(GAIN_FEED))
    middle_grad_ref[0] = middle_grad
    branch_grad = (small(SCALE_ATTENTION) * middle_grad).astype(low)
    branch_grad_ref[0] = branch_grad
    sums_ref[0:1] += rows_sum(cotangent * lowered)
    sums_ref[1:2] += rows_sum((small(SCALE_FEED) * cotangent).astype(low).astype(jnp.float32))
    sums_ref[2:3] += rows_sum(grad * hat)
    sums_ref[3:4] += rows_sum(grad)
    sums_ref[4:5] += rows_sum(middle_grad * branch)
    sums_ref[5:6] += rows_sum(branch_grad.astype(jnp.float32))

    @pl.when(pl.program_id(0) == 0)
    def _():
        finish(out_w, sem)

    above = dot(branch_grad, out_w[...], 1, 1).astype(low)
    width = key_ref.shape[2] // probs_ref.shape[1]
    for quad in range(probs_ref.shape[1]):
        lanes = slice(width * quad, width * (quad + 1))
        probs_low = probs_ref[0, quad]
        probs = probs_low.astype(jnp.float32)
        heads = by_head(above[:, lanes])
        probs_grad = dot(value_ref[0, :, lanes], heads, 1, 1)
        inner = rows_sum(probs_grad * probs)
        score_grad = (probs * (probs_grad - inner)).astype(low)
        value_grad[0, :, lanes] = dot(probs_low, heads).astype(low)
        key_grad[0, :, lanes] = (dot(score_grad, by_head(query_ref[0, :, lanes])) * factor).astype(low)
        query_grad[0, :, lanes] = (from_heads(dot(score_grad, key_ref[0, :, lanes], 0, 0)) * factor).astype(low)


def input_back_kernel(parts_a, parts_b, *refs):
    slots_ref, query_grad, key_grad, value_grad, key_hat_ref, value_hat_ref, key_scale_ref, value_scale_ref = refs[:8]
    middle_grad_ref, mixed_ref, small_ref = refs[8:11]
    part_a, part_b, refs = refs[11 : 11 + parts_a], refs[11 + parts_a : 11 + parts_a + parts_b], refs[11 + parts_a + parts_b :]
    masked_ref, latent_ref, away_ref, sums_ref, query_w, key_w, value_w, sems = refs[-8:]

    @pl.when(pl.program_id(0) == 0)
    def _():
        for index, (parts, tile, whole) in enumerate(((part_a, 0, query_w), (part_a, 1, key_w), (part_b, 0, value_w))):
            fetch(slots_ref, units_of(parts, tile), whole, sems.at[index])
        for index, whole in enumerate((query_w, key_w, value_w)):
            finish(whole, sems.at[index])

    small = lambda row: small_ref[row : row + 1]
    count = query_grad.shape[1]

    @pl.when(pl.program_id(0) == 0)
    def _():
        sums_ref[...] = jnp.zeros_like(sums_ref)

    key_hat, key_scale = key_hat_ref[0], key_scale_ref[0]
    query_hat = key_hat[:count]
    value_hat = value_hat_ref[0]
    from_query = dot(query_grad[0], query_w[...], 1, 1)
    from_key = dot(key_grad[0], key_w[...], 1, 1)
    from_value = dot(value_grad[0], value_w[...], 1, 1)
    sums_ref[0:1] += rows_sum(from_query * query_hat)
    sums_ref[1:2] += rows_sum(from_query)
    sums_ref[2:3] += rows_sum(from_key * key_hat)
    sums_ref[3:4] += rows_sum(from_value * value_hat)
    sums_ref[4:5] += rows_sum(from_value)
    sums_ref[5:6] += rows_sum(wide(query_grad.at[0]))
    sums_ref[6:7] += rows_sum(wide(value_grad.at[0]))
    both = standard_back(from_key, key_hat, key_scale, small(GAIN_KEY)) + standard_back(
        from_value, value_hat, value_scale_ref[0], small(GAIN_VALUE)
    )
    query_part = standard_back(from_query, query_hat, key_scale[:count], small(GAIN_QUERY))
    masked = middle_grad_ref[0] + query_part + both[:count]
    size, visible = masked_ref.shape[1], latent_ref.shape[1]
    starts, _ = layout(visible, size)
    masked_ref[0] = masked[:size]
    latent_ref[0] = both[starts[2] : starts[2] + visible]
    away_ref[0, :size] = masked[size:].astype(away_ref.dtype)
    away_ref[0, size : 2 * size] = mixed_ref[0]
    away_ref[0, 2 * size :] = both[starts[3] : starts[3] + visible].astype(away_ref.dtype)


def weights_back_kernel(
    out_slots_ref, attended, branch_grad, value_normed, value_grad, key_normed, key_grad, query_normed, query_grad,
    keep_a, send_a, keep_b, send_b, *refs,
):
    inputs = (attended, branch_grad, value_normed, value_grad, key_normed, key_grad, query_normed, query_grad)
    held, wholes, sems = refs[:8], refs[8:12], refs[12]
    copies = [pltpu.make_async_copy(ref, scratch, sems.at[4 + k]) for k, (ref, scratch) in enumerate(zip(inputs, held))]
    for copy in copies:
        copy.start()
    targets = ((keep_b, send_b, 1), (keep_b, send_b, 0), (keep_a, send_a, 1), (keep_a, send_a, 0))
    for index, (keep, send, tile) in enumerate(targets):
        copies[2 * index].wait()
        copies[2 * index + 1].wait()
        wholes[index][...] = dot(held[2 * index][...], held[2 * index + 1][...], 0, 0).astype(jnp.bfloat16)
        store(out_slots_ref, wholes[index], [keep.at[tile], send.at[tile]], sems.at[index])
    for index in range(4):
        finish(wholes[index], sems.at[index])


def call(name, kernel, grid, ins, outs, operands, scratch=(), after=(), us=1):
    ins = list(ins) + [ANY] * len(after)
    operands = tuple(operands) + tuple(after)

    def spec(entry, shape):
        if entry is None:
            return pl.BlockSpec(shape, lambda *i: (0,) * len(shape))
        if entry is ANY or entry is SMEM:
            return pl.BlockSpec(memory_space=entry)
        return pl.BlockSpec(*entry)

    return pl.pallas_call(
        kernel,
        name=name,
        grid=grid,
        in_specs=[spec(entry, operand.shape) for entry, operand in zip(ins, operands, strict=True)],
        out_specs=[spec(entry, shape) for entry, shape, _ in outs],
        out_shape=[jax.ShapeDtypeStruct(shape, dtype) for _, shape, dtype in outs],
        scratch_shapes=list(scratch),
        compiler_params=pltpu.CompilerParams(vmem_limit_bytes=56 << 20),
        cost_estimate=pl.CostEstimate(flops=int(us * 1.1e9), bytes_accessed=int(us * 3.5e6), transcendentals=0),
    )(*operands)


def by_crop(shape):
    block = (1,) + tuple(shape[1:])
    return block, lambda i: (i,) + (0,) * (len(block) - 1)


def pack_kernel(vectors, *refs):
    *in_refs, out_ref = refs
    low = jnp.bfloat16
    parts = [wide(ref) for ref in in_refs[vectors + bool(vectors) :]]
    if vectors:
        device_ref, thin, bias_ref = in_refs[0], in_refs[1:vectors], in_refs[vectors]
        width = out_ref.shape[1]
        device = device_ref[0]
        shard, half = thin[0].shape[0], bias_ref.shape[0] // 2
        rows = jnp.concatenate(
            [pad_lanes(wide(ref).reshape(1, -1), 128) for ref in thin]
            + [jnp.zeros((BIAS_ROW - len(thin), 128), jnp.float32)], axis=0
        )
        value = lax.broadcasted_iota(jnp.int32, (128, width), 0)
        lane = lax.broadcasted_iota(jnp.int32, (128, width), 1)
        there = (lane == shard * device + value) & (value < shard)
        line = [dot(rows.astype(low), jnp.where(there, 1.0, 0.0).astype(low))]
        bias = jnp.broadcast_to(pad_lanes(wide(bias_ref).reshape(1, -1), 128), (8, 128)).astype(low)
        row = lax.broadcasted_iota(jnp.int32, (8, width), 0)
        strips = jnp.zeros((8, width), jnp.float32)
        column = half * (2 * lax.div(device, 4) + lax.rem(device, 2))
        for part in range(2):
            inside = (value >= half * part) & (value < half * (part + 1))
            there = (lane == column + value - half * part) & inside
            spot = row == 2 * part + lax.rem(lax.div(device, 2), 2)
            strips = jnp.where(spot, dot(bias, jnp.where(there, 1.0, 0.0).astype(low)), strips)
        middle = len(parts) // 2
        parts = parts[:middle] + line + [strips] + parts[middle:]
    out_ref[...] = jnp.concatenate(parts, axis=0).astype(out_ref.dtype)


def pad_lanes(rows, width):
    if rows.shape[1] == width:
        return rows
    return jnp.concatenate([rows, jnp.zeros((rows.shape[0], width - rows.shape[1]), rows.dtype)], axis=1)


def pack(parts, device=None, vectors=()):
    width, dtype = parts[0].shape[1], parts[0].dtype
    first = (device.reshape(1), *vectors) if vectors else ()
    ins = [SMEM] + [None] * len(vectors) if vectors else []
    run = lambda operands: call(
        "pack", functools.partial(pack_kernel, len(vectors)), (), ins + [None] * len(operands),
        [(None, (sum(part.shape[0] for part in operands) + LINE_ROWS * bool(vectors), width), dtype)], (*first, *operands), us=1,
    )[0]
    if all(part.shape[0] % 8 == 0 for part in parts):
        return run(parts)
    if not vectors:
        return jnp.concatenate(parts)
    half = len(parts) // 2
    blank = jnp.zeros((8, width), dtype)
    line = run([blank, blank])[8 : 8 + LINE_ROWS]
    return jnp.concatenate([*parts[:half], line, *parts[half:]])


def stage(*values):
    return lax.optimization_barrier(values)


def position_table(width):
    quarter = width // 4
    frequency = 10000.0 ** (-np.arange(quarter) / quarter)
    angle = np.arange(16)[:, None] * frequency
    wave = np.concatenate([np.sin(angle), np.cos(angle)], axis=1)
    table = np.zeros((32, width))
    table[:16, : width // 2] = wave
    table[16:, width // 2 :] = wave
    table = table.astype(np.float32)
    high = table.astype(ml_dtypes.bfloat16)
    low = (table - high.astype(np.float32)).astype(ml_dtypes.bfloat16)
    return np.concatenate([high, low])


def local(
    latents, queries, order, weight_query, bias_query, weight_key, weight_value, bias_value, weight_out, bias_out,
    gain_query, shift_query, gain_key, gain_value, shift_value, scale_attention, weight_up, bias_up, weight_down,
    bias_down, gain_feed, shift_feed, scale_feed, cotangent,
):
    low = jnp.bfloat16
    net = Net()
    slot = lax.axis_index("query")
    crops = latents.shape[0] // 2
    visible, masked = latents.shape[1], queries.shape[1]
    shard, width = weight_query.shape
    count = net.count
    _, rows = layout(visible, masked)
    block = lambda values, which: lax.dynamic_slice_in_dim(values, which * crops, crops, 0)
    own_latents, own_queries, own_cot = [block(v, slot) for v in (latents, queries, cotangent)]
    vectors = [
        bias_query, bias_value, bias_out, gain_query, shift_query, gain_key, gain_value, shift_value, scale_attention,
        bias_down, gain_feed, shift_feed, scale_feed, bias_up,
    ]
    device = (2 * (4 * net.at_ring + 2 * net.at_x + net.at_core) + slot).astype(jnp.int32)
    deep = weight_down.shape[0]
    half = deep // 2
    f32 = jnp.float32
    ring = net.ring
    pairs = 2 * ring
    flat = lambda values: values.reshape(-1, values.shape[-1])

    own_a = pack([weight_query, weight_key, weight_value, weight_out], device, vectors)
    turn_all = lambda value: [("turn", value, step) for step in range(1, ring)]
    away = jnp.concatenate([block(values, 1 - slot) for values in (queries, cotangent, latents)], axis=1)
    (*rings_a, came), (own_a, weight_up, weight_down, own_cot, order) = net.moves(
        [*turn_all(own_a), ("y", away)], own_a, weight_up, weight_down, own_cot, order
    )
    rings_a = [own_a, *rings_a]
    ups = jnp.moveaxis(weight_up.reshape(shard, pairs, 2, 2, 2, half), (2, 4), (0, 1)).reshape(2, 2, shard, width)
    up_own = lax.dynamic_index_in_dim(ups, net.at_core, 0, keepdims=False)
    up_came = net.swap_core(lax.dynamic_index_in_dim(ups, 1 - net.at_core, 0, keepdims=False))
    table = jnp.asarray(position_table(width))
    own_order = block(order, slot)
    part = lambda start, size, which: lax.dynamic_slice_in_dim(own_order, start + which * size, size, 1)
    gap = jnp.full((crops, rows // 2 - masked - visible), -1, jnp.int32)
    indices = jnp.concatenate(
        [
            part(2 * visible, masked, slot), part(2 * visible, masked, 1 - slot),
            part(0, visible, slot), gap, part(0, visible, 1 - slot), gap,
        ],
        axis=1,
    )
    steps = jnp.stack([indices // GRID, jnp.where(indices < 0, -1, indices % GRID)], axis=-1)
    own_b, own_c = [pack([weight_down[half * k : half * (k + 1)], up_own[k], up_came[k]]) for k in range(2)]
    rings_a, came, own_b, own_c, steps = stage(rings_a, came, own_b, own_c, steps)

    cut = 2 * shard
    line = sum(piece[cut : cut + LINE_ROWS] for piece in rings_a[1:]) + rings_a[0][cut : cut + LINE_ROWS]
    one = jnp.concatenate([piece[:cut] for piece in rings_a] + [line])
    two = jnp.stack([piece[cut + LINE_ROWS :] for piece in rings_a])
    (*rings_b, one_x, two_y), (own_b, one, two, came) = net.moves(
        [*turn_all(own_b), ("x", one), ("y", two)], own_b, one, two, came
    )
    crop_out = lambda shape, dtype: (by_crop(shape), shape, dtype)
    wide_shape, thin_shape = (crops, rows, width), (crops, rows, 1)
    operands = (steps, own_queries, own_latents, came, table)
    key_hat, value_hat, key_scale, value_scale = call(
        "prepare", prepare_kernel, (crops,), [by_crop(a.shape) for a in operands[:4]] + [None],
        [crop_out(wide_shape, f32)] * 2 + [crop_out(thin_shape, f32)] * 2, operands, scratch=[pltpu.VMEM((rows, width), f32)],
    )
    one_x, two_y, rings_b, key_hat, value_hat, key_scale, value_scale = stage(
        one_x, two_y, [own_b, *rings_b], key_hat, value_hat, key_scale, value_scale
    )

    line = one[ring * cut :] + one_x[ring * cut :]
    one = jnp.concatenate([one[: ring * cut], one_x[: ring * cut], line])
    two = net.pair(two, two_y, 2)
    (*rings_c, one_y, two_x), (own_c, one, two) = net.moves([*turn_all(own_c), ("y", one), ("x", two)], own_c, one, two)
    one_y, two_x, rings_c = stage(one_y, two_x, [own_c, *rings_c])

    line = one[pairs * cut :] + one_y[pairs * cut :]
    units = lambda values: values[: pairs * cut].reshape(pairs, cut, width)
    one = net.pair(units(one), units(one_y), 2)
    pieces = list(zip(rings_b, rings_c))
    downs = jnp.stack([jnp.concatenate([b[:half], c[:half]]) for b, c in pieces])
    ups = jnp.stack([jnp.concatenate([b[half:], c[half:]]) for b, c in pieces])
    sends = [("core", value) for value in (one, two, two_x, line)]
    (downs_x, ups_y, one_core, two_core, two_x_core, line_core), (one, two, two_x, line, downs, ups) = net.moves(
        [("x", downs), ("y", ups), *sends], one, two, two_x, line, downs, ups
    )
    part_a, part_b = [one, one_core], [two, two_x, two_core, two_x_core]
    small = line.astype(f32) + line_core.astype(f32)
    part_a, part_b, small = stage(part_a, part_b, small)
    (part_a, places), (part_b, _) = net.aligned(part_a, net.units), net.aligned(part_b, net.units)
    slots, out_places = net.slots(width)
    ask_shape = (crops, 2 * masked, width)
    dma = pltpu.SemaphoreType.DMA
    square_vmem = pltpu.VMEM((width, width), low)
    quads = HEADS // GROUP
    factor = (width // HEADS) ** -0.5
    probs_shape = (crops, quads, rows, GROUP * 2 * masked)
    of_came = lambda part: ((1, masked, width), lambda i: (i, part, 0))
    operands = (places, key_hat, value_hat, own_queries, came, small, *part_a, *part_b)
    parts = len(part_a) + len(part_b)
    query_p, key_p, value_p, probs, attended, branch, feed_hat, feed_scale, feed, *normed = call(
        "attend", functools.partial(attend_kernel, visible, factor, len(part_a), len(part_b)), (crops,),
        [SMEM] + [by_crop(a.shape) for a in operands[1:4]] + [of_came(0), None] + [ANY] * parts,
        [
            crop_out(ask_shape, low), crop_out(wide_shape, low), crop_out(wide_shape, low), crop_out(probs_shape, low),
            crop_out(ask_shape, low), crop_out(ask_shape, f32), crop_out(ask_shape, f32),
            crop_out((crops, 2 * masked, 1), f32), crop_out(ask_shape, low),
            crop_out(ask_shape, low), crop_out(wide_shape, low), crop_out(wide_shape, low),
        ],
        operands, scratch=[square_vmem] * 4 + [dma((4,))],
    )
    downs_x, ups_y, query_p, key_p, value_p, probs, attended, branch, feed_hat, feed_scale, feed, normed = stage(
        downs_x, ups_y, query_p, key_p, value_p, probs, attended, branch, feed_hat, feed_scale, feed, normed
    )

    def second_of(k):
        own, other = slice(half * k, half * (k + 1)), slice(2 * shard * k, 2 * shard * (k + 1))
        return jnp.concatenate([downs[:, own], downs_x[:, own]]), net.pair(ups[:, other], ups_y[:, other], 2)

    feed = flat(feed)
    down_b, up_b = second_of(0)
    (down_b_y, up_b_x, feed_other, *other_cot), (down_b, up_b, feed, own_cot, came) = net.moves(
        [("y", down_b), ("x", up_b), ("core", feed), ("core", own_cot), ("core", came)], down_b, up_b, feed, own_cot, came
    )
    down_c, up_c = second_of(1)
    down_b_y, up_b_x, feed_other, other_cot, down_c, up_c = stage(down_b_y, up_b_x, feed_other, other_cot, down_c, up_c)
    parts_b, where_b = net.feed_units((down_b, down_b_y, up_b, up_b_x), pairs)
    (down_c_y, up_c_x), (down_c, up_c, parts_b) = net.moves([("y", down_c), ("x", up_c)], down_c, up_c, parts_b)
    asks = crops * 2 * masked
    core = net.at_core.reshape(1).astype(jnp.int32)
    aligned = slots == net.units and half % 16 == 0
    down_out_places = out_places[:pairs] // 2 if aligned else out_places

    def feed_call(name, parts, where, last):
        down_plan, down_places, up_plan, up_places = where
        operands = (
            up_places, down_places, out_places, down_out_places, core, feed, feed_other, own_cot, came, *other_cot, small,
        )
        of_cot = ((crops, masked, width), lambda i: (0, 1, 0))
        ins = [SMEM] * 5 + [None] * 3 + [of_cot, None, of_cot, None] + [ANY] * len(parts)
        down_shape = (1, 2, ring, half, width) if aligned else (1, slots // 2, width // slots, width)
        outs = [(ANY, down_shape, low)] * 2 + [(ANY, (2, slots // 2, width // slots, width), low), (None, (1, width), f32)]
        outs += [(None, (asks, width), f32)] * 2 + [(None, (asks if last else 2 * asks, width), low)] * (1 + last)
        return call(
            name, functools.partial(feed_kernel, last, down_plan, up_plan, len(parts)), (1,), ins, outs,
            (*operands, *parts), scratch=[square_vmem] * 4 + [dma((4,))],
        )

    def feed_grads(keep, send, up):
        if aligned:
            keep, send = jnp.moveaxis(keep, 1, 2), jnp.moveaxis(send, 1, 2)
            up = up.reshape(2, pairs, 2, shard, width)
        else:
            down = jnp.concatenate([keep, send], axis=1).reshape(1, pairs, 2, half, width)[:, net.scattered[:pairs] // 2]
            keep, send = down[:, :ring], down[:, ring:]
            up = up.reshape(net.units, 2, shard, width)[net.scattered].reshape(2, pairs, 2, shard, width)
        return net.feed_second(keep, send, up)

    down_keep, down_send, up_out, bias_b, *partial_b = feed_call("feed0", parts_b, where_b, 0)
    down_c_y, up_c_x, down_keep, down_send, up_out, bias_b, partial_b = stage(
        down_c_y, up_c_x, down_keep, down_send, up_out, bias_b, partial_b
    )

    parts_c, where_c = net.feed_units((down_c, down_c_y, up_c, up_c_x), pairs)
    kept_b, sends = feed_grads(down_keep, down_send, up_out)
    (swapped_b, *came_b), (kept_b, partial_b, parts_c) = net.moves(
        [("core", partial_b[2]), *sends], kept_b, partial_b, parts_c
    )
    down_keep, down_send, up_out, bias_c, *partial_c = feed_call("feed1", parts_c, where_c, 1)
    swapped_c = [net.swap_core(values) for values in partial_c[2:]]
    came_b, down_keep, down_send, up_out, bias_c, swapped_b, partial_c, swapped_c = stage(
        came_b, down_keep, down_send, up_out, bias_c, swapped_b, partial_c, swapped_c
    )
    of_crops = lambda values: values.reshape(ask_shape)
    swapped = [swapped_b.reshape(2 * crops, *ask_shape[1:]), *[of_crops(values) for values in swapped_c]]
    partials = [of_crops(values) for values in (partial_b[0], partial_c[0], partial_b[1], partial_c[1])]

    kept_c, sends = feed_grads(down_keep, down_send, up_out)
    came_c, (kept_c, partials, swapped) = net.moves(sends, kept_c, partials, swapped)
    operands = (
        places, query_p, key_p, value_p, probs, *partials[:2], *swapped[:2], *partials[2:], swapped[0], swapped[2],
        own_cot, came, own_queries, came, branch, feed_hat, feed_scale, small, *part_b,
    )
    of_swapped = lambda part: [((1, *ask_shape[1:]), lambda i: (i + part * crops, 0, 0)), by_crop(ask_shape)]
    masked_shape, latent_shape = (crops, masked, width), (crops, visible, width)
    sums_out = (None, (8, width), f32)
    mixed_own, mixed_came, middle_grad, branch_grad, feed_sums, query_grad, key_grad, value_grad = call(
        "attend_back", functools.partial(attend_back_kernel, factor, len(part_b)), (crops,),
        [SMEM] + [by_crop(a.shape) for a in operands[1:7]] + of_swapped(0) + [by_crop(ask_shape)] * 2 + of_swapped(1)
        + [by_crop(own_cot.shape), of_came(1), by_crop(own_queries.shape), of_came(0)]
        + [by_crop(a.shape) for a in operands[17:20]] + [None] + [ANY] * len(part_b),
        [
            crop_out(masked_shape, low), crop_out(masked_shape, low), crop_out(ask_shape, f32), crop_out(ask_shape, low),
            sums_out, crop_out(ask_shape, low), crop_out(wide_shape, low), crop_out(wide_shape, low),
        ],
        operands, scratch=[square_vmem, dma(())],
    )
    came_c, mixed_own, mixed_came, middle_grad, branch_grad, feed_sums, query_grad, key_grad, value_grad = stage(
        came_c, mixed_own, mixed_came, middle_grad, branch_grad, feed_sums, query_grad, key_grad, value_grad
    )

    kept_b, sends_b = net.scatter_third(kept_b, came_b)
    kept_c, sends_c = net.scatter_third(kept_c, came_c)
    came, (kept_b, kept_c, query_grad, key_grad, value_grad) = net.moves(
        [*sends_b, *sends_c], kept_b, kept_c, query_grad, key_grad, value_grad
    )
    came_b, came_c = came[:2], came[2:]
    operands = (
        attended, branch_grad, normed[2], value_grad, normed[1], key_grad, normed[0], query_grad,
    )
    operands = [flat(operand) for operand in operands]
    keep_a, send_a, keep_b, send_b = call(
        "weights_back", weights_back_kernel, (), [SMEM] + [ANY] * 8,
        [(ANY, (2, slots // 2, width // slots, width), low)] * 4, (out_places, *operands),
        scratch=[pltpu.VMEM(operand.shape, low) for operand in operands] + [square_vmem] * 4 + [dma((12,))],
    )
    came_b, came_c, keep_a, send_a, keep_b, send_b = stage(came_b, came_c, keep_a, send_a, keep_b, send_b)

    (keep_a, send_a), (keep_b, send_b) = net.unaligned(keep_a, send_a), net.unaligned(keep_b, send_b)
    came, (keep_a, keep_b, query_grad, key_grad, value_grad) = net.moves(
        [("core", send_a), ("core", send_b)], keep_a, keep_b, query_grad, key_grad, value_grad
    )
    first_a = (keep_a, keep_b, *came)
    operands = (
        places, query_grad, key_grad, value_grad, key_hat, value_hat, key_scale, value_scale, middle_grad, mixed_came, small,
        *part_a, *part_b,
    )
    home_rows = 2 * masked + visible
    masked_own, latent_own, away, input_sums = call(
        "input_back", functools.partial(input_back_kernel, len(part_a), len(part_b)), (crops,),
        [SMEM] + [by_crop(a.shape) for a in operands[1:10]] + [None] + [ANY] * parts,
        [
            crop_out(masked_shape, f32), crop_out(latent_shape, f32), crop_out((crops, home_rows, width), low), sums_out,
        ],
        operands, scratch=[square_vmem] * 3 + [dma((3,))],
    )
    masked_own, latent_own, away, input_sums, first_a = stage(masked_own, latent_own, away, input_sums, first_a)

    kept_a, sends_a = net.scatter_second(first_a)
    (shape_b, kept_b), sends_b = net.scatter_fourth(kept_b, came_b)
    strips = jnp.arange(LINE_ROWS - BIAS_ROW)[:, None]
    strips = jnp.where(strips == net.at_core, bias_b, 0.0) + jnp.where(strips == 2 + net.at_core, bias_c, 0.0)
    lines = jnp.concatenate([input_sums, feed_sums, strips])
    came, (kept_a, kept_b, lines) = net.moves([*sends_a, *sends_b, ("core", lines)], kept_a, kept_b, lines)
    came, = stage(came)
    came_a, came_b, line_core = came[:2], came[2:-1], came[-1]

    kept_a, sends_a = net.scatter_third(kept_a, came_a)
    (shape_c, kept_c), sends_c = net.scatter_fourth(kept_c, came_c)
    lines = lines + line_core
    (line_y, *came), (kept_a, kept_c, lines) = net.moves([("y", lines), *sends_a, *sends_c], kept_a, kept_c, lines)
    came_a, came_c = came[:2], came[2:]
    lines = lines + line_y
    lines = lines + net.swap_x(lines)
    came_a, came_c, lines = stage(came_a, came_c, lines)

    (shape_a, kept_a), sends_a = net.scatter_fourth(kept_a, came_a)
    sends_a = [(kind, jnp.concatenate([piece, lines.astype(low)]), step) for kind, piece, step in sends_a]
    (home_rows, *came_a), (kept_a, lines, came_b, came_c) = net.moves(
        [("y", away), *sends_a], kept_a, lines, came_b, came_c
    )
    lines = sum((piece[-LINE_ROWS:].astype(f32) for piece in came_a), lines)
    came_a = [piece[:-LINE_ROWS] for piece in came_a]
    down_sums, up_sums = zip(
        net.scatter_last((shape_b, kept_b), came_b), net.scatter_last((shape_c, kept_c), came_c)
    )
    down_sum = jnp.concatenate([down[0] for down in down_sums])
    up_sums = jnp.stack([up.reshape(2, shard, width) for up in up_sums])
    up_came = net.swap_core(up_sums[:, 1])
    up_sums = jnp.where(net.at_core == 0, jnp.stack([up_sums[:, 0], up_came]), jnp.stack([up_came, up_sums[:, 0]]))
    up_sum = jnp.moveaxis(up_sums.reshape(2, 2, shard, pairs, 2, half), (0, 1), (2, 4)).reshape(shard, count * deep)
    sum_a, sum_b = net.scatter_last((shape_a, kept_a), came_a)
    sum_b = sum_b.reshape(sum_a.shape)

    vector = lax.dynamic_slice(lines, (0, shard * device), (BIAS_ROW, shard))
    column = half * (2 * (device // 4) + device % 2)
    strip = lambda k: lax.dynamic_slice(lines, (BIAS_ROW + 2 * k + net.at_core, column), (1, half))
    bias_up_sum = jnp.concatenate([strip(0)[0], strip(1)[0]])

    def home(keep, came, dtype):
        keep, came = keep.astype(dtype), came.astype(dtype)
        return jnp.concatenate([jnp.where(slot == 0, keep, came), jnp.where(slot == 0, came, keep)], axis=0)

    return (
        home(mixed_own, home_rows[:, masked : 2 * masked], low),
        home(latent_own, home_rows[:, 2 * masked :], f32),
        home(masked_own, home_rows[:, :masked], f32),
        sum_a[0],
        vector[5],
        sum_a[1],
        sum_b[0],
        vector[6],
        sum_b[1],
        vector[13],
        vector[0],
        vector[1],
        vector[2],
        vector[3],
        vector[4],
        vector[12],
        up_sum,
        bias_up_sum,
        down_sum,
        vector[9],
        vector[10],
        vector[11],
        vector[8],
    )


def solution(mesh):
    batch, query = mesh.devices.shape
    split = Mesh(mesh.devices.reshape(batch // 4, 2, 2, query), (*BATCH, "query"))
    crop, rows, flat = P(BATCH, "query", None), P((*BATCH, "query"), None), P((*BATCH, "query"))
    in_specs = (crop, crop, P(BATCH, None), rows, flat, rows, rows, flat, rows, *[flat] * 7, rows, flat, rows, *[flat] * 4, crop)
    out_specs = (crop, crop, crop, rows, flat, rows, rows, flat, rows, *[flat] * 7, rows, flat, rows, *[flat] * 4)
    return jax.shard_map(local, mesh=split, in_specs=in_specs, out_specs=out_specs, check_vma=False)
```

profile of v0, /device:TPU:0, one launch (start us, length us, event | category | flops | bytes accessed | tf_op | source)
XLA Modules:
  0.0 256.7 jit_solution(11745980602067623508)
XLA Ops:
  6.9 2.6 %collective-permute-start.3 = (bf16[3,146,768]{2,1,0:T(8,128)(2,1)S(1)}, bf16[3,146,768]{2,1,0:T(8,128)(2,1)S(1)}, u32[]{:S(2)}, u32[]{:S(2)}) collective-permute-start(bf16[3,146,768]{2,1,0:T(8,128)(2,1)S(1)} %pad_maximum_fusion.5), channel_id=1, source_target_pairs={{0,1},{1,0},{2,3},{3,2},{4,5},{5,4},{6,7},{7,6},{8,9},{9,8},{10,11... | collective-permute-start | bytes 2018312 | tf_op jit(solution)/shard_map/ppermute | solution.py:67
  11.0 2.6 %collective-permute-start.1 = (bf16[120,768]{1,0:T(8,128)(2,1)S(1)}, bf16[120,768]{1,0:T(8,128)(2,1)S(1)}, u32[]{:S(2)}, u32[]{:S(2)}) collective-permute-start(bf16[120,768]{1,0:T(8,128)(2,1)S(1)} %copy-done.41), channel_id=1, source_target_pairs={{0,16},{8,24},{16,0},{24,8},{1,17},{9,25},{17,1},{25,9},{2,18},{10... | collective-permute-start | bytes 552968 | tf_op jit(solution)/shard_map/ppermute | solution.py:55
  20.4 5.6 %collective-permute-done.1 = bf16[120,768]{1,0:T(8,128)(2,1)S(1)} collective-permute-done((bf16[120,768]{1,0:T(8,128)(2,1)S(1)}, bf16[120,768]{1,0:T(8,128)(2,1)S(1)}, u32[]{:S(2)}, u32[]{:S(2)}) %collective-permute-start.1) | collective-permute-done | bytes 184352 | tf_op jit(solution)/shard_map/ppermute | solution.py:55
  29.2 3.5 %collective-permute-start.7 = (bf16[96,768]{1,0:T(8,128)(2,1)S(1)}, bf16[96,768]{1,0:T(8,128)(2,1)S(1)}, u32[]{:S(2)}, u32[]{:S(2)}) collective-permute-start(bf16[96,768]{1,0:T(8,128)(2,1)S(1)} %copy-done.44), channel_id=1, source_target_pairs={{0,8},{8,16},{16,24},{24,0},{1,9},{9,17},{17,25},{25,1},{2,10},{10... | collective-permute-start | bytes 442376 | tf_op jit(solution)/shard_map/ppermute | solution.py:55
  36.0 5.1 %prepare.1 = (f32[3,208,768]{2,1,0:T(8,128)}, f32[3,208,768]{2,1,0:T(8,128)}, f32[3,208,1]{2,1,0:T(8,128)}, f32[3,208,1]{2,1,0:T(8,128)}) custom-call(s32[3,208,2]{2,1,0:T(8,128)} %copy.105.place_ref, bf16[3,48,768]{2,1,0:T(8,128)(2,1)} %get-tuple-element.645.own_ref.refs_3_.refs_15_, bf16[3,50,768]{2,1,0:T(8,128)(2,1)} %get-tuple-element.643.own_latent_ref, ...), custom_call_target="tpu_custom_call" | custom-call | flops 1100000000 | bytes 3500000 | tf_op jit(solution)/shard_map/prepare/pallas_call | solution.py:492
  46.1 3.5 %collective-permute-start.12 = (bf16[96,768]{1,0:T(8,128)(2,1)S(1)}, bf16[96,768]{1,0:T(8,128)(2,1)S(1)}, u32[]{:S(2)}, u32[]{:S(2)}) collective-permute-start(bf16[96,768]{1,0:T(8,128)(2,1)S(1)} %copy-done.43), channel_id=1, source_target_pairs={{0,8},{8,16},{16,24},{24,0},{1,9},{9,17},{17,25},{25,1},{2,10},{10... | collective-permute-start | bytes 442376 | tf_op jit(solution)/shard_map/ppermute | solution.py:55
  52.1 3.7 %collective-permute-done.12 = bf16[96,768]{1,0:T(8,128)(2,1)S(1)} collective-permute-done((bf16[96,768]{1,0:T(8,128)(2,1)S(1)}, bf16[96,768]{1,0:T(8,128)(2,1)S(1)}, u32[]{:S(2)}, u32[]{:S(2)}) %collective-permute-start.12) | collective-permute-done | bytes 147488 | tf_op jit(solution)/shard_map/ppermute | solution.py:55
  55.8 4.2 %collective-permute-done.13 = bf16[96,768]{1,0:T(8,128)(2,1)S(1)} collective-permute-done((bf16[96,768]{1,0:T(8,128)(2,1)S(1)}, bf16[96,768]{1,0:T(8,128)(2,1)S(1)}, u32[]{:S(2)}, u32[]{:S(2)}) %collective-permute-start.13) | collective-permute-done | bytes 147488 | tf_op jit(solution)/shard_map/ppermute | solution.py:55
  69.1 12.0 %attend.1 = (bf16[3,96,768]{2,1,0:T(8,128)(2,1)}, bf16[3,208,768]{2,1,0:T(8,128)(2,1)}, bf16[3,208,768]{2,1,0:T(8,128)(2,1)}, bf16[3,3,208,384]{3,2,1,0:T(8,128)...) custom-call(s32[16]{0:T(128)} %fusion.16.refs_0_, ...), custom_call_target="tpu_custom_call" | custom-call | flops 1100000000 | bytes 3500000 | tf_op jit(solution)/shard_map/attend/pallas_call | solution.py:492
  86.8 11.6 %collective-permute-done.21 = bf16[8,48,768]{2,1,0:T(8,128)(2,1)S(1)} collective-permute-done((bf16[8,48,768]{2,1,0:T(8,128)(2,1)S(1)}, bf16[8,48,768]{2,1,0:T(8,128)(2,1)S(1)}, u32[]{:S(2)}, u32[]{:S(2)}) %collective-permute-start.21) | collective-permute-done | bytes 589856 | tf_op jit(solution)/shard_map/ppermute | solution.py:67
  103.6 10.1 %feed0.1 = (bf16[1,2,4,48,768]{4,3,2,1,0:T(8,128)(2,1)}, bf16[1,2,4,48,768]{4,3,2,1,0:T(8,128)(2,1)}, bf16[2,8,48,768]{3,2,1,0:T(8,128)(2,1)}, f32[1,768]{1,0:T(...) custom-call(s32[16]{0:T(128)} %fusion.16.refs_0_, s32[8]{0:T(128)} %get-tuple-element.732.refs_1_, ...), custom_call_target="tpu_custom_call" | custom-call | flops 1100000000 | bytes 3500000 | tf_op jit(solution)/shard_map/feed0/pallas_call | solution.py:492
  113.7 2.6 %collective-permute-done.26 = bf16[8,48,768]{2,1,0:T(8,128)(2,1)S(1)} collective-permute-done((bf16[8,48,768]{2,1,0:T(8,128)(2,1)}, bf16[8,48,768]{2,1,0:T(8,128)(2,1)S(1)}, u32[]{:S(2)}, u32[]{:S(2)}) %collective-permute-start.26) | collective-permute-done | bytes 589856 | tf_op jit(solution)/shard_map/ppermute | solution.py:67
  122.7 10.1 %feed1.1 = (bf16[1,2,4,48,768]{4,3,2,1,0:T(8,128)(2,1)}, bf16[1,2,4,48,768]{4,3,2,1,0:T(8,128)(2,1)}, bf16[2,8,48,768]{3,2,1,0:T(8,128)(2,1)}, f32[1,768]{1,0:T(...) custom-call(s32[16]{0:T(128)} %fusion.16.refs_0_, ...), custom_call_target="tpu_custom_call" | custom-call | flops 1100000000 | bytes 3500000 | tf_op jit(solution)/shard_map/feed1/pallas_call | solution.py:492
  143.9 11.2 %attend_back.1 = (bf16[3,48,768]{2,1,0:T(8,128)(2,1)}, bf16[3,48,768]{2,1,0:T(8,128)(2,1)}, f32[3,96,768]{2,1,0:T(8,128)}, bf16[3,96,768]{2,1,0:T(8,128)(2,1)}, ...) custom-call(s32[16]{0:T(128)} %fusion.16.refs_0_, ...), custom_call_target="tpu_custom_call" | custom-call | flops 1100000000 | bytes 3500000 | tf_op jit(solution)/shard_map/attend_back/pallas_call | solution.py:492
  162.5 7.8 %weights_back.1 = (bf16[2,8,48,768]{3,2,1,0:T(8,128)(2,1)}, bf16[2,8,48,768]{3,2,1,0:T(8,128)(2,1)}, bf16[2,8,48,768]{3,2,1,0:T(8,128)(2,1)}, bf16[2,8,48,768]{3,2,1,0:T(8,128)(2,1)}) custom-call(s32[16]{0:T(128)} %copy-done.56, bf16[288,768]{1,0:T(8,128)(2,1)} %bitcast.279, bf16[288,768]{1,0:T(8,128)(2,1)} %bitcast.281, bf16[624,768]{1,0:T(8,128)(2,1)} %bitcast.264, ...), custom_call_target="tpu_custom_call" | custom-call | flops 1100000000 | bytes 3500000 | tf_op jit(solution)/shard_map/weights_back/pallas_call | solution.py:492
  176.4 10.0 %input_back.1 = (f32[3,48,768]{2,1,0:T(8,128)}, f32[3,50,768]{2,1,0:T(8,128)}, bf16[3,146,768]{2,1,0:T(8,128)(2,1)}, f32[8,768]{1,0:T(8,128)}) custom-call(s32[16]{0:T(128)} %fusion.16.refs_0_, bf16[3,96,768]{2,1,0:T(8,128)(2,1)} %get-tuple-element.521.refs_1_, bf16[3,208,768]{2,1,0:T(8,128)(2,1)} %get-tuple-element.522.refs_2_, ...), custom_call_target="tpu_custom_call" | custom-call | flops 1100000000 | bytes 3500000 | tf_op jit(solution)/shard_map/input_back/pallas_call | solution.py:492
  193.5 3.7 %collective-permute-start.43 = (bf16[96,768]{1,0:T(8,128)(2,1)S(1)}, bf16[96,768]{1,0:T(8,128)(2,1)S(1)}, u32[]{:S(2)}, u32[]{:S(2)}) collective-permute-start(bf16[96,768]{1,0:T(8,128)(2,1)S(1)} %pad_maximum_fusion.24), channel_id=1, source_target_pairs={{0,8},{8,16},{16,24},{24,0},{1,9},{9,17},{17,25},{25,1},{2,10},{10... | collective-permute-start | bytes 442376 | tf_op jit(solution)/shard_map/ppermute | solution.py:55
  199.9 3.4 %collective-permute-done.43 = bf16[96,768]{1,0:T(8,128)(2,1)S(1)} collective-permute-done((bf16[96,768]{1,0:T(8,128)(2,1)S(1)}, bf16[96,768]{1,0:T(8,128)(2,1)S(1)}, u32[]{:S(2)}, u32[]{:S(2)}) %collective-permute-start.43) | collective-permute-done | bytes 147488 | tf_op jit(solution)/shard_map/ppermute | solution.py:55
  203.2 6.1 %collective-permute-done.44 = bf16[96,768]{1,0:T(8,128)(2,1)S(1)} collective-permute-done((bf16[96,768]{1,0:T(8,128)(2,1)S(1)}, bf16[96,768]{1,0:T(8,128)(2,1)S(1)}, u32[]{:S(2)}, u32[]{:S(2)}) %collective-permute-start.44) | collective-permute-done | bytes 147488 | tf_op jit(solution)/shard_map/ppermute | solution.py:55
  215.5 3.6 %collective-permute-start.49 = (bf16[96,768]{1,0:T(8,128)(2,1)S(1)}, bf16[96,768]{1,0:T(8,128)(2,1)S(1)}, u32[]{:S(2)}, u32[]{:S(2)}) collective-permute-start(bf16[96,768]{1,0:T(8,128)(2,1)S(1)} %pad_maximum_fusion.27), channel_id=1, source_target_pairs={{0,8},{8,16},{16,24},{24,0},{1,9},{9,17},{17,25},{25,1},{2,10},{10... | collective-permute-start | bytes 442376 | tf_op jit(solution)/shard_map/ppermute | solution.py:55
  221.6 4.1 %collective-permute-start.51 = (bf16[96,768]{1,0:T(8,128)(2,1)S(1)}, bf16[96,768]{1,0:T(8,128)(2,1)S(1)}, u32[]{:S(2)}, u32[]{:S(2)}) collective-permute-start(bf16[96,768]{1,0:T(8,128)(2,1)S(1)} %pad_maximum_fusion.29), channel_id=1, source_target_pairs={{0,24},{8,0},{16,8},{24,16},{1,25},{9,1},{17,9},{25,17},{2,26},{10... | collective-permute-start | bytes 442376 | tf_op jit(solution)/shard_map/ppermute | solution.py:55
  228.2 2.7 %collective-permute-done.51 = bf16[96,768]{1,0:T(8,128)(2,1)S(1)} collective-permute-done((bf16[96,768]{1,0:T(8,128)(2,1)S(1)}, bf16[96,768]{1,0:T(8,128)(2,1)S(1)}, u32[]{:S(2)}, u32[]{:S(2)}) %collective-permute-start.51) | collective-permute-done | bytes 147488 | tf_op jit(solution)/shard_map/ppermute | solution.py:55
  241.7 7.0 %collective-permute-done.56 = bf16[120,768]{1,0:T(8,128)(2,1)S(1)} collective-permute-done((bf16[120,768]{1,0:T(8,128)(2,1)S(1)}, bf16[120,768]{1,0:T(8,128)(2,1)S(1)}, u32[]{:S(2)}, u32[]{:S(2)}) %collective-permute-start.56) | collective-permute-done | bytes 184352 | tf_op jit(solution)/shard_map/ppermute | solution.py:55
  250.8 2.6 %collective-permute-done.54 = bf16[3,146,768]{2,1,0:T(8,128)(2,1)S(1)} collective-permute-done((bf16[3,146,768]{2,1,0:T(8,128)(2,1)}, bf16[3,146,768]{2,1,0:T(8,128)(2,1)S(1)}, u32[]{:S(2)}, u32[]{:S(2)}) %collective-permute-start.54) | collective-permute-done | bytes 672800 | tf_op jit(solution)/shard_map/ppermute | solution.py:67
  (394 shorter events, 115.0 us)
Async XLA Ops:
  6.9 19.2 %collective-permute-start.3 = (bf16[3,146,768]{2,1,0:T(8,128)(2,1)S(1)}, bf16[3,146,768]{2,1,0:T(8,128)(2,1)S(1)}, u32[]{:S(2)}, u32[]{:S(2)}) collective-permute-start(bf16[3,146,768]{2,1,0:T(8,128)(2,1)S(1)} %pad_maximum_fusion.5), channel_id=1, source_target_pairs={{0,1},{1,0},{2,3},{3,2},{4,5},{5,4},{6,7},{7,6},{8,9},{9,8},{10,11... | collective-permute-start | bytes 2018312 | tf_op jit(solution)/shard_map/ppermute | solution.py:67
  11.0 15.0 %collective-permute-start.1 = (bf16[120,768]{1,0:T(8,128)(2,1)S(1)}, bf16[120,768]{1,0:T(8,128)(2,1)S(1)}, u32[]{:S(2)}, u32[]{:S(2)}) collective-permute-start(bf16[120,768]{1,0:T(8,128)(2,1)S(1)} %copy-done.41), channel_id=1, source_target_pairs={{0,16},{8,24},{16,0},{24,8},{1,17},{9,25},{17,1},{25,9},{2,18},{10... | collective-permute-start | bytes 552968 | tf_op jit(solution)/shard_map/ppermute | solution.py:55
  26.2 16.9 %collective-permute-start.5 = (bf16[216,768]{1,0:T(8,128)(2,1)S(1)}, bf16[216,768]{1,0:T(8,128)(2,1)S(1)}, u32[]{:S(2)}, u32[]{:S(2)}) collective-permute-start(bf16[216,768]{1,0:T(8,128)(2,1)S(1)} %add_dynamic-update-slice_fusion), channel_id=1, source_target_pairs={{0,4},{4,0},{1,5},{5,1},{2,6},{6,2},{3,7},{7,3},{8,12},{12,8},{9,1... | collective-permute-start | bytes 995336 | tf_op jit(solution)/shard_map/ppermute | solution.py:61
  27.8 15.3 %collective-permute-start.6 = (bf16[4,48,768]{2,1,0:T(8,128)(2,1)S(1)}, bf16[4,48,768]{2,1,0:T(8,128)(2,1)S(1)}, u32[]{:S(2)}, u32[]{:S(2)}) collective-permute-start(bf16[4,48,768]{2,1,0:T(8,128)(2,1)S(1)} %pad_maximum_fusion.15), channel_id=1, source_target_pairs={{0,1},{1,0},{2,3},{3,2},{4,5},{5,4},{6,7},{7,6},{8,9},{9,8},{10,11... | collective-permute-start | bytes 884744 | tf_op jit(solution)/shard_map/ppermute | solution.py:67
  44.0 16.5 %collective-permute-start.10 = (bf16[408,768]{1,0:T(8,128)(2,1)S(1)}, bf16[408,768]{1,0:T(8,128)(2,1)S(1)}, u32[]{:S(2)}, u32[]{:S(2)}) collective-permute-start(bf16[408,768]{1,0:T(8,128)(2,1)S(1)} %pad_maximum_fusion.6), channel_id=1, source_target_pairs={{0,1},{1,0},{2,3},{3,2},{4,5},{5,4},{6,7},{7,6},{8,9},{9,8},{10,11... | collective-permute-start | bytes 1880072 | tf_op jit(solution)/shard_map/ppermute | solution.py:67
  45.6 14.9 %collective-permute-start.11 = (bf16[4,2,48,768]{3,2,1,0:T(8,128)(2,1)S(1)}, bf16[4,2,48,768]{3,2,1,0:T(8,128)(2,1)S(1)}, u32[]{:S(2)}, u32[]{:S(2)}) collective-permute-start(bf16[4,2,48,768]{3,2,1,0:T(8,128)(2,1)S(1)} %bitcast.222), channel_id=1, source_target_pairs={{0,4},{4,0},{1,5},{5,1},{2,6},{6,2},{3,7},{7,3},{8,12},{12,8},{9,1... | collective-permute-start | bytes 1769480 | tf_op jit(solution)/shard_map/ppermute | solution.py:61
  62.9 18.3 %collective-permute-start.15 = (bf16[4,96,768]{2,1,0:T(8,128)(2,1)S(1)}, bf16[4,96,768]{2,1,0:T(8,128)(2,1)S(1)}, u32[]{:S(2)}, u32[]{:S(2)}) collective-permute-start(bf16[4,96,768]{2,1,0:T(8,128)(2,1)S(1)} %pad_maximum_fusion.8), channel_id=1, source_target_pairs={{0,4},{4,0},{1,5},{5,1},{2,6},{6,2},{3,7},{7,3},{8,12},{12,8},{9,1... | collective-permute-start | bytes 1769480 | tf_op jit(solution)/shard_map/ppermute | solution.py:61
  64.7 16.4 %collective-permute-start.16 = (bf16[4,96,768]{2,1,0:T(8,128)(2,1)S(1)}, bf16[4,96,768]{2,1,0:T(8,128)(2,1)S(1)}, u32[]{:S(2)}, u32[]{:S(2)}) collective-permute-start(bf16[4,96,768]{2,1,0:T(8,128)(2,1)S(1)} %pad_maximum_fusion.9), channel_id=1, source_target_pairs={{0,1},{1,0},{2,3},{3,2},{4,5},{5,4},{6,7},{7,6},{8,9},{9,8},{10,11... | collective-permute-start | bytes 1769480 | tf_op jit(solution)/shard_map/ppermute | solution.py:67
  82.7 16.4 %collective-permute-start.25 = (bf16[3,146,768]{2,1,0:T(8,128)(2,1)S(1)}, bf16[3,146,768]{2,1,0:T(8,128)(2,1)S(1)}, u32[]{:S(2)}, u32[]{:S(2)}) collective-permute-start(bf16[3,146,768]{2,1,0:T(8,128)(2,1)S(1)} %copy-done.1), channel_id=1, source_target_pairs={{0,2},{2,0},{1,3},{3,1},{4,6},{6,4},{5,7},{7,5},{8,10},{10,8},{9,1... | collective-permute-start | bytes 2018312 | tf_op jit(solution)/shard_map/ppermute | solution.py:64
  82.7 15.7 %collective-permute-start.21 = (bf16[8,48,768]{2,1,0:T(8,128)(2,1)S(1)}, bf16[8,48,768]{2,1,0:T(8,128)(2,1)S(1)}, u32[]{:S(2)}, u32[]{:S(2)}) collective-permute-start(bf16[8,48,768]{2,1,0:T(8,128)(2,1)S(1)} %pad_maximum_fusion.10), channel_id=1, source_target_pairs={{0,1},{1,0},{2,3},{3,2},{4,5},{5,4},{6,7},{7,6},{8,9},{9,8},{10,11... | collective-permute-start | bytes 1769480 | tf_op jit(solution)/shard_map/ppermute | solution.py:67
  83.6 15.5 %collective-permute-start.22 = (bf16[4,2,48,768]{3,2,1,0:T(8,128)(2,1)S(1)}, bf16[4,2,48,768]{3,2,1,0:T(8,128)(2,1)S(1)}, u32[]{:S(2)}, u32[]{:S(2)}) collective-permute-start(bf16[4,2,48,768]{3,2,1,0:T(8,128)(2,1)S(1)} %bitcast.246), channel_id=1, source_target_pairs={{0,4},{4,0},{1,5},{5,1},{2,6},{6,2},{3,7},{7,3},{8,12},{12,8},{9,1... | collective-permute-start | bytes 1769480 | tf_op jit(solution)/shard_map/ppermute | solution.py:61
  101.4 14.9 %collective-permute-start.26 = (bf16[8,48,768]{2,1,0:T(8,128)(2,1)}, bf16[8,48,768]{2,1,0:T(8,128)(2,1)S(1)}, u32[]{:S(2)}, u32[]{:S(2)}) collective-permute-start(bf16[8,48,768]{2,1,0:T(8,128)(2,1)} %pad_maximum_fusion.12), channel_id=1, source_target_pairs={{0,1},{1,0},{2,3},{3,2},{4,5},{5,4},{6,7},{7,6},{8,9},{9,8},{10,11... | collective-permute-start | bytes 1769480 | tf_op jit(solution)/shard_map/ppermute | solution.py:67
  102.5 14.4 %collective-permute-start.27 = (bf16[4,2,48,768]{3,2,1,0:T(8,128)(2,1)S(1)}, bf16[4,2,48,768]{3,2,1,0:T(8,128)(2,1)S(1)}, u32[]{:S(2)}, u32[]{:S(2)}) collective-permute-start(bf16[4,2,48,768]{3,2,1,0:T(8,128)(2,1)S(1)} %bitcast.244), channel_id=1, source_target_pairs={{0,4},{4,0},{1,5},{5,1},{2,6},{6,2},{3,7},{7,3},{8,12},{12,8},{9,1... | collective-permute-start | bytes 1769480 | tf_op jit(solution)/shard_map/ppermute | solution.py:61
  120.7 16.1 %collective-permute-start.30 = (bf16[576,768]{1,0:T(8,128)(2,1)S(1)}, bf16[576,768]{1,0:T(8,128)(2,1)S(1)}, u32[]{:S(2)}, u32[]{:S(2)}) collective-permute-start(bf16[576,768]{1,0:T(8,128)(2,1)S(1)} %copy-done.60), channel_id=1, source_target_pairs={{0,2},{2,0},{1,3},{3,1},{4,6},{6,4},{5,7},{7,5},{8,10},{10,8},{9,1... | collective-permute-start | bytes 2654216 | tf_op jit(solution)/shard_map/ppermute | solution.py:64
  120.7 15.7 %collective-permute-start.28 = (bf16[1,4,2,48,768]{4,3,1,2,0:T(8,128)(2,1)S(1)}, bf16[1,4,2,48,768]{4,3,1,2,0:T(8,128)(2,1)S(1)}, u32[]{:S(2)}, u32[]{:S(2)}) collective-permute-start(bf16[1,4,2,48,768]{4,3,1,2,0:T(8,128)(2,1)S(1)} %bitcast.296), channel_id=1, source_target_pairs={{0,4},{4,0},{1,5},{5,1},{2,6},{6,2},{3,7},{7,3},{8,12},{12,8},{9,1... | collective-permute-start | bytes 1769480 | tf_op jit(solution)/shard_map/ppermute | solution.py:61
  121.3 15.5 %collective-permute-start.29 = (bf16[2,8,24,768]{3,2,0,1:T(8,128)(2,1)S(1)}, bf16[2,8,24,768]{3,2,0,1:T(8,128)(2,1)S(1)}, u32[]{:S(2)}, u32[]{:S(2)}) collective-permute-start(bf16[2,8,24,768]{3,2,0,1:T(8,128)(2,1)S(1)} %copy_bitcast_fusion), channel_id=1, source_target_pairs={{0,1},{1,0},{2,3},{3,2},{4,5},{5,4},{6,7},{7,6},{8,9},{9,8},{10,11... | collective-permute-start | bytes 1769480 | tf_op jit(solution)/shard_map/ppermute | solution.py:67
  139.1 16.3 %collective-permute-start.33 = (bf16[1,4,2,48,768]{4,3,1,2,0:T(8,128)(2,1)}, bf16[1,4,2,48,768]{4,3,1,2,0:T(8,128)(2,1)}, u32[]{:S(2)}, u32[]{:S(2)}) collective-permute-start(bf16[1,4,2,48,768]{4,3,1,2,0:T(8,128)(2,1)} %bitcast.53), channel_id=1, source_target_pairs={{0,4},{4,0},{1,5},{5,1},{2,6},{6,2},{3,7},{7,3},{8,12},{12,8},{9,1... | collective-permute-start | bytes 1769480 | tf_op jit(solution)/shard_map/ppermute | solution.py:61
  140.5 14.9 %collective-permute-start.34 = (bf16[2,8,24,768]{3,2,1,0:T(8,128)(2,1)}, bf16[2,8,24,768]{3,2,1,0:T(8,128)(2,1)}, u32[]{:S(2)}, u32[]{:S(2)}) collective-permute-start(bf16[2,8,24,768]{3,2,1,0:T(8,128)(2,1)} %dynamic-slice_bitcast_fusion), channel_id=1, source_target_pairs={{0,1},{1,0},{2,3},{3,2},{4,5},{5,4},{6,7},{7,6},{8,9},{9,8},{10,11... | collective-permute-start | bytes 1769480 | tf_op jit(solution)/shard_map/ppermute | solution.py:67
  191.2 18.1 %collective-permute-start.41 = (bf16[2,4,2,24,768]{4,3,0,1,2:T(8,128)(2,1)S(1)}, bf16[2,4,2,24,768]{4,3,0,1,2:T(8,128)(2,1)S(1)}, u32[]{:S(2)}, u32[]{:S(2)}) collective-permute-start(bf16[2,4,2,24,768]{4,3,0,1,2:T(8,128)(2,1)S(1)} %add_convert_fusion.1), channel_id=1, source_target_pairs={{0,4},{4,0},{1,5},{5,1},{2,6},{6,2},{3,7},{7,3},{8,12},{12,8},{9,1... | collective-permute-start | bytes 1769480 | tf_op jit(solution)/shard_map/ppermute | solution.py:61
  192.1 17.2 %collective-permute-start.42 = (bf16[2,8,24,768]{3,2,0,1:T(8,128)(2,1)S(1)}, bf16[2,8,24,768]{3,2,0,1:T(8,128)(2,1)S(1)}, u32[]{:S(2)}, u32[]{:S(2)}) collective-permute-start(bf16[2,8,24,768]{3,2,0,1:T(8,128)(2,1)S(1)} %fusion.1), channel_id=1, source_target_pairs={{0,1},{1,0},{2,3},{3,2},{4,5},{5,4},{6,7},{7,6},{8,9},{9,8},{10,11... | collective-permute-start | bytes 1769480 | tf_op jit(solution)/shard_map/ppermute | solution.py:67
  210.4 20.6 %collective-permute-start.47 = (bf16[2,4,24,768]{3,2,0,1:T(8,128)(2,1)S(1)}, bf16[2,4,24,768]{3,2,0,1:T(8,128)(2,1)S(1)}, u32[]{:S(2)}, u32[]{:S(2)}) collective-permute-start(bf16[2,4,24,768]{3,2,0,1:T(8,128)(2,1)S(1)} %fusion.10), channel_id=1, source_target_pairs={{0,1},{1,0},{2,3},{3,2},{4,5},{5,4},{6,7},{7,6},{8,9},{9,8},{10,11... | collective-permute-start | bytes 884744 | tf_op jit(solution)/shard_map/ppermute | solution.py:67
  211.7 19.3 %collective-permute-start.48 = (bf16[2,4,24,768]{3,2,0,1:T(8,128)(2,1)S(1)}, bf16[2,4,24,768]{3,2,0,1:T(8,128)(2,1)S(1)}, u32[]{:S(2)}, u32[]{:S(2)}) collective-permute-start(bf16[2,4,24,768]{3,2,0,1:T(8,128)(2,1)S(1)} %fusion.7), channel_id=1, source_target_pairs={{0,4},{4,0},{1,5},{5,1},{2,6},{6,2},{3,7},{7,3},{8,12},{12,8},{9,1... | collective-permute-start | bytes 884744 | tf_op jit(solution)/shard_map/ppermute | solution.py:61
  232.8 15.9 %collective-permute-start.56 = (bf16[120,768]{1,0:T(8,128)(2,1)S(1)}, bf16[120,768]{1,0:T(8,128)(2,1)S(1)}, u32[]{:S(2)}, u32[]{:S(2)}) collective-permute-start(bf16[120,768]{1,0:T(8,128)(2,1)S(1)} %get-tuple-element.598), channel_id=1, source_target_pairs={{0,16},{8,24},{16,0},{24,8},{1,17},{9,25},{17,1},{25,9},{2,18},{10... | collective-permute-start | bytes 552968 | tf_op jit(solution)/shard_map/ppermute | solution.py:55
  235.7 17.7 %collective-permute-start.54 = (bf16[3,146,768]{2,1,0:T(8,128)(2,1)}, bf16[3,146,768]{2,1,0:T(8,128)(2,1)S(1)}, u32[]{:S(2)}, u32[]{:S(2)}) collective-permute-start(bf16[3,146,768]{2,1,0:T(8,128)(2,1)} %get-tuple-element.593), channel_id=1, source_target_pairs={{0,1},{1,0},{2,3},{3,2},{4,5},{5,4},{6,7},{7,6},{8,9},{9,8},{10,11... | collective-permute-start | bytes 2018312 | tf_op jit(solution)/shard_map/ppermute | solution.py:67
  (100 other events, 697.4 us)
where the time goes:
time: 258 us; the launch traced here: 257 us
  Pallas kernels  71.4 us (28%)
  starting transfers between devices  67.7 us (26%)
  waiting for transfers between devices  64.7 us (25%)
  local copies, waits for them, and re-layouts  31.3 us (12%)
  other arithmetic  19.2 us (7%)
    pallas_call x10, Pallas kernels, call(): pl.pallas_call(kernel, name=name, grid=grid, in_specs=[spec(entry, operan...  71.4 us
    ppermute x18, starting transfers between devices, turn(): lax.ppermute(values, 'ring', [(place, (place + step) % self.ring) for pla...  36.4 us
    ppermute x18, waiting for transfers between devices, turn(): lax.ppermute(values, 'ring', [(place, (place + step) % self.ring) for pla...  36.1 us
    ppermute x14, waiting for transfers between devices, swap_y(): return lax.ppermute(values, 'query', [(0, 1), (1, 0)])  21 us
    ppermute x14, starting transfers between devices, swap_y(): return lax.ppermute(values, 'query', [(0, 1), (1, 0)])  17.5 us
    unnamed x124, local copies, waits for them, and re-layouts  12.4 us
    ppermute x12, starting transfers between devices, swap_x(): return lax.ppermute(values, 'x', [(0, 1), (1, 0)])  10.7 us
  transfers between devices with their start and end apart: 59, of which 25 were waited for; matrix products, arithmetic and copies ran while one was open for 7% of the time, Pallas kernels for 27%

commit v1 on v0

--- a/solution.py
+++ b/solution.py
@@ -15,6 +15,7 @@
 HEADS = 12
 GRID = 14
 GROUP = 4
+PACK_MIB = 16
 CHUNK = 768
 EPSILON = 1e-06
 BIAS_QUERY = 0
@@ -94,11 +95,15 @@
 
     def feed_units(self, following, units):
         down, down_y, up, up_x = following
-        down_parts, down_places = self.aligned([self.pair(down, down_y, 1)], units)
+        if down.shape[1] % 16 == 0:
+            down_parts, places = [down[:, None], down_y[:, None]], 2 * (self.gathered[:units] // 2)
+            down_places = jnp.concatenate([places + self.at_y, places + 1 - self.at_y]).astype(jnp.int32)
+        else:
+            down_parts, down_places = self.aligned([self.pair(down, down_y, 1)], units)
         up_parts, up_places = self.aligned_cores([up, up_x])
-        down_plan = [(0, (index, 0)) for index in range(down_parts[0].shape[0])]
+        down_plan = [(part, (index, 0)) for part, array in enumerate(down_parts) for index in range(array.shape[0])]
         up_plan = [
-            (1 + part, (index, tile))
+            (len(down_parts) + part, (index, tile))
             for tile in range(up_parts[0].shape[1]) for part, array in enumerate(up_parts) for index in range(array.shape[0])
         ]
         return [*down_parts, *up_parts], (down_plan, down_places, up_plan, up_places)
@@ -478,14 +483,14 @@
         finish(wholes[index], sems.at[index])
 
 
-def call(name, kernel, grid, ins, outs, operands, scratch=(), after=(), us=1):
+def call(name, kernel, grid, ins, outs, operands, scratch=(), after=(), us=1, mib=54):
     ins = list(ins) + [ANY] * len(after)
     operands = tuple(operands) + tuple(after)
 
     def spec(entry, shape):
         if entry is None:
             return pl.BlockSpec(shape, lambda *i: (0,) * len(shape))
-        if entry is ANY or entry is SMEM:
+        if entry in (ANY, SMEM, pltpu.HBM):
             return pl.BlockSpec(memory_space=entry)
         return pl.BlockSpec(*entry)
 
@@ -493,11 +498,11 @@
         kernel,
         name=name,
         grid=grid,
-        in_specs=[spec(entry, operand.shape) for entry, operand in zip(ins, operands, strict=True)],
+        in_specs=[spec(pltpu.HBM if entry is ANY else entry, operand.shape) for entry, operand in zip(ins, operands, strict=True)],
         out_specs=[spec(entry, shape) for entry, shape, _ in outs],
         out_shape=[jax.ShapeDtypeStruct(shape, dtype) for _, shape, dtype in outs],
         scratch_shapes=list(scratch),
-        compiler_params=pltpu.CompilerParams(vmem_limit_bytes=56 << 20),
+        compiler_params=pltpu.CompilerParams(vmem_limit_bytes=mib << 20),
         cost_estimate=pl.CostEstimate(flops=int(us * 1.1e9), bytes_accessed=int(us * 3.5e6), transcendentals=0),
     )(*operands)
 
@@ -550,7 +555,7 @@
     ins = [SMEM] + [None] * len(vectors) if vectors else []
     run = lambda operands: call(
         "pack", functools.partial(pack_kernel, len(vectors)), (), ins + [None] * len(operands),
-        [(None, (sum(part.shape[0] for part in operands) + LINE_ROWS * bool(vectors), width), dtype)], (*first, *operands), us=1,
+        [(None, (sum(part.shape[0] for part in operands) + LINE_ROWS * bool(vectors), width), dtype)], (*first, *operands), mib=PACK_MIB,
     )[0]
     if all(part.shape[0] % 8 == 0 for part in parts):
         return run(parts)
@@ -644,7 +649,7 @@
     operands = (steps, own_queries, own_latents, came, table)
     key_hat, value_hat, key_scale, value_scale = call(
         "prepare", prepare_kernel, (crops,), [by_crop(a.shape) for a in operands[:4]] + [None],
-        [crop_out(wide_shape, f32)] * 2 + [crop_out(thin_shape, f32)] * 2, operands, scratch=[pltpu.VMEM((rows, width), f32)],
+        [crop_out(wide_shape, f32)] * 2 + [crop_out(thin_shape, f32)] * 2, operands, scratch=[pltpu.VMEM((rows, width), f32)], mib=54,
     )
     one_x, two_y, rings_b, key_hat, value_hat, key_scale, value_scale = stage(
         one_x, two_y, [own_b, *rings_b], key_hat, value_hat, key_scale, value_scale
@@ -824,23 +829,29 @@
     strips = jnp.where(strips == net.at_core, bias_b, 0.0) + jnp.where(strips == 2 + net.at_core, bias_c, 0.0)
     lines = jnp.concatenate([input_sums, feed_sums, strips])
     came, (kept_a, kept_b, lines) = net.moves([*sends_a, *sends_b, ("core", lines)], kept_a, kept_b, lines)
-    came, = stage(came)
-    came_a, came_b, line_core = came[:2], came[2:-1], came[-1]
+    lines = lines + came[-1]
+    line_y = net.swap_y(lines)
+    came, lines, line_y = stage(came[:-1], lines, line_y)
+    came_a, came_b = came[:2], came[2:]
 
     kept_a, sends_a = net.scatter_third(kept_a, came_a)
     (shape_c, kept_c), sends_c = net.scatter_fourth(kept_c, came_c)
-    lines = lines + line_core
-    (line_y, *came), (kept_a, kept_c, lines) = net.moves([("y", lines), *sends_a, *sends_c], kept_a, kept_c, lines)
-    came_a, came_c = came[:2], came[2:]
     lines = lines + line_y
-    lines = lines + net.swap_x(lines)
-    came_a, came_c, lines = stage(came_a, came_c, lines)
-
+    high = lines.astype(low)
+    rest = (lines - high.astype(f32)).astype(low)
+    ridden = jnp.concatenate([flat(sends_a[1][1]), high, rest])
+    shape = sends_a[1][1].shape
+    came, (kept_a, kept_c, lines) = net.moves([("x", ridden), sends_a[0], *sends_c], kept_a, kept_c, lines)
+    came_x, came_c = came[0], came[2:]
+    line_x = came_x[-2 * LINE_ROWS : -LINE_ROWS].astype(f32) + came_x[-LINE_ROWS:].astype(f32)
+    came_a = (came[1], came_x[: -2 * LINE_ROWS].reshape(shape))
+    lines = lines + line_x
+    came_a, lines, away = stage(came_a, lines, away)
+
+    home_rows = net.swap_y(away)
     (shape_a, kept_a), sends_a = net.scatter_fourth(kept_a, came_a)
     sends_a = [(kind, jnp.concatenate([piece, lines.astype(low)]), step) for kind, piece, step in sends_a]
-    (home_rows, *came_a), (kept_a, lines, came_b, came_c) = net.moves(
-        [("y", away), *sends_a], kept_a, lines, came_b, came_c
-    )
+    came_a, (kept_a, lines, came_b, came_c) = net.moves(sends_a, kept_a, lines, came_b, came_c)
     lines = sum((piece[-LINE_ROWS:].astype(f32) for piece in came_a), lines)
     came_a = [piece[:-LINE_ROWS] for piece in came_a]
     down_sums, up_sums = zip(

time: 258 us -> 252 us (0.977)
  Pallas kernels: 71.4 us -> 66.6 us
    pallas_call x10, Pallas kernels: 71.4 us -> 66.6 us  [call(): pl.pallas_call(kernel, name=name, grid=grid, in_specs=[spec(pltpu.HBM if...]
    ppermute x18, waiting for transfers between devices: 36.1 us -> 38.9 us  [turn(): lax.ppermute(values, 'ring', [(place, (place + step) % self.ring) for pla...]
    ppermute x12 -> x11, waiting for transfers between devices: 4.1 us -> 5.25 us  [swap_x(): return lax.ppermute(values, 'x', [(0, 1), (1, 0)])]
    ppermute x12 -> x11, starting transfers between devices: 10.7 us -> 11.1 us  [swap_x(): return lax.ppermute(values, 'x', [(0, 1), (1, 0)])]
    unnamed x124 -> x156, local copies, waits for them, and re-layouts: 12.4 us -> 12.2 us
  transfers between devices with their start and end apart: 59 -> 58, of which waited for: 25 -> 25; matrix products, arithmetic and copies ran while one was open for 7% -> 7% of each run, Pallas kernels for 27% -> 26%
where the time goes in v1:
time: 252 us; the launch traced here: 251 us
  starting transfers between devices  67.3 us (27%)
  Pallas kernels  66.6 us (26%)
  waiting for transfers between devices  66.1 us (26%)
  local copies, waits for them, and re-layouts  30.2 us (12%)
  other arithmetic  18.3 us (7%)
  between operations  2.62 us (1%)
    pallas_call x10, Pallas kernels, call(): pl.pallas_call(kernel, name=name, grid=grid, in_specs=[spec(pltpu.HBM if...  66.6 us
    ppermute x18, waiting for transfers between devices, turn(): lax.ppermute(values, 'ring', [(place, (place + step) % self.ring) for pla...  38.9 us
    ppermute x18, starting transfers between devices, turn(): lax.ppermute(values, 'ring', [(place, (place + step) % self.ring) for pla...  36 us
    ppermute x14, waiting for transfers between devices, swap_y(): return lax.ppermute(values, 'query', [(0, 1), (1, 0)])  19 us
    ppermute x14, starting transfers between devices, swap_y(): return lax.ppermute(values, 'query', [(0, 1), (1, 0)])  17.2 us
    unnamed x156, local copies, waits for them, and re-layouts  12.2 us
    ppermute x11, starting transfers between devices, swap_x(): return lax.ppermute(values, 'x', [(0, 1), (1, 0)])  11.1 us
    ppermute x11, waiting for transfers between devices, swap_x(): return lax.ppermute(values, 'x', [(0, 1), (1, 0)])  5.25 us
  transfers between devices with their start and end apart: 58, of which 25 were waited for; matrix products, arithmetic and copies ran while one was open for 7% of the time, Pallas kernels for 26%

profile of v1, /device:TPU:0, one launch (start us, length us, event | category | flops | bytes accessed | tf_op | source)
XLA Modules:
  0.0 251.1 jit_solution(7800000488325722959)
XLA Ops:
  6.2 2.6 %collective-permute-start.3 = (bf16[3,146,768]{2,1,0:T(8,128)(2,1)S(1)}, bf16[3,146,768]{2,1,0:T(8,128)(2,1)S(1)}, u32[]{:S(2)}, u32[]{:S(2)}) collective-permute-start(bf16[3,146,768]{2,1,0:T(8,128)(2,1)S(1)} %pad_maximum_fusion.3), channel_id=1, source_target_pairs={{0,1},{1,0},{2,3},{3,2},{4,5},{5,4},{6,7},{7,6},{8,9},{9,8},{10,11... | collective-permute-start | bytes 2018312 | tf_op jit(solution)/shard_map/ppermute | solution.py:68
  10.4 2.6 %collective-permute-start.1 = (bf16[120,768]{1,0:T(8,128)(2,1)S(1)}, bf16[120,768]{1,0:T(8,128)(2,1)S(1)}, u32[]{:S(2)}, u32[]{:S(2)}) collective-permute-start(bf16[120,768]{1,0:T(8,128)(2,1)S(1)} %pack.3), channel_id=1, source_target_pairs={{0,16},{8,24},{16,0},{24,8},{1,17},{9,25},{17,1},{25,9},{2,18},{10... | collective-permute-start | bytes 552968 | tf_op jit(solution)/shard_map/ppermute | solution.py:56
  14.8 3.4 %collective-permute-done = bf16[120,768]{1,0:T(8,128)(2,1)S(1)} collective-permute-done((bf16[120,768]{1,0:T(8,128)(2,1)S(1)}, bf16[120,768]{1,0:T(8,128)(2,1)S(1)}, u32[]{:S(2)}, u32[]{:S(2)}) %collective-permute-start) | collective-permute-done | bytes 184352 | tf_op jit(solution)/shard_map/ppermute | solution.py:56
  18.2 7.2 %collective-permute-done.1 = bf16[120,768]{1,0:T(8,128)(2,1)S(1)} collective-permute-done((bf16[120,768]{1,0:T(8,128)(2,1)S(1)}, bf16[120,768]{1,0:T(8,128)(2,1)S(1)}, u32[]{:S(2)}, u32[]{:S(2)}) %collective-permute-start.1) | collective-permute-done | bytes 184352 | tf_op jit(solution)/shard_map/ppermute | solution.py:56
  28.6 3.5 %collective-permute-start.7 = (bf16[96,768]{1,0:T(8,128)(2,1)S(1)}, bf16[96,768]{1,0:T(8,128)(2,1)S(1)}, u32[]{:S(2)}, u32[]{:S(2)}) collective-permute-start(bf16[96,768]{1,0:T(8,128)(2,1)S(1)} %pack.4), channel_id=1, source_target_pairs={{0,8},{8,16},{16,24},{24,0},{1,9},{9,17},{17,25},{25,1},{2,10},{10... | collective-permute-start | bytes 442376 | tf_op jit(solution)/shard_map/ppermute | solution.py:56
  35.3 5.1 %prepare.1 = (f32[3,208,768]{2,1,0:T(8,128)}, f32[3,208,768]{2,1,0:T(8,128)}, f32[3,208,1]{2,1,0:T(8,128)}, f32[3,208,1]{2,1,0:T(8,128)}) custom-call(s32[3,208,2]{2,1,0:T(8,128)} %copy.113.place_ref, bf16[3,48,768]{2,1,0:T(8,128)(2,1)} %get-tuple-element.644.own_ref.refs_3_.refs_15_, bf16[3,50,768]{2,1,0:T(8,128)(2,1)} %get-tuple-element.642.own_latent_ref, ...), custom_call_target="tpu_custom_call" | custom-call | flops 1100000000 | bytes 3500000 | tf_op jit(solution)/shard_map/prepare/pallas_call | solution.py:497
  46.5 3.6 %collective-permute-start.12 = (bf16[96,768]{1,0:T(8,128)(2,1)S(1)}, bf16[96,768]{1,0:T(8,128)(2,1)S(1)}, u32[]{:S(2)}, u32[]{:S(2)}) collective-permute-start(bf16[96,768]{1,0:T(8,128)(2,1)S(1)} %pack.5), channel_id=1, source_target_pairs={{0,8},{8,16},{16,24},{24,0},{1,9},{9,17},{17,25},{25,1},{2,10},{10... | collective-permute-start | bytes 442376 | tf_op jit(solution)/shard_map/ppermute | solution.py:56
  52.6 3.6 %collective-permute-done.12 = bf16[96,768]{1,0:T(8,128)(2,1)S(1)} collective-permute-done((bf16[96,768]{1,0:T(8,128)(2,1)S(1)}, bf16[96,768]{1,0:T(8,128)(2,1)S(1)}, u32[]{:S(2)}, u32[]{:S(2)}) %collective-permute-start.12) | collective-permute-done | bytes 147488 | tf_op jit(solution)/shard_map/ppermute | solution.py:56
  56.1 4.4 %collective-permute-done.13 = bf16[96,768]{1,0:T(8,128)(2,1)S(1)} collective-permute-done((bf16[96,768]{1,0:T(8,128)(2,1)S(1)}, bf16[96,768]{1,0:T(8,128)(2,1)S(1)}, u32[]{:S(2)}, u32[]{:S(2)}) %collective-permute-start.13) | collective-permute-done | bytes 147488 | tf_op jit(solution)/shard_map/ppermute | solution.py:56
  70.2 12.0 %attend.1 = (bf16[3,96,768]{2,1,0:T(8,128)(2,1)}, bf16[3,208,768]{2,1,0:T(8,128)(2,1)}, bf16[3,208,768]{2,1,0:T(8,128)(2,1)}, bf16[3,3,208,384]{3,2,1,0:T(8,128)...) custom-call(s32[16]{0:T(128)} %fusion.16.refs_0_, ...), custom_call_target="tpu_custom_call" | custom-call | flops 1100000000 | bytes 3500000 | tf_op jit(solution)/shard_map/attend/pallas_call | solution.py:497
  89.7 11.6 %collective-permute-done.21 = bf16[8,48,768]{2,1,0:T(8,128)(2,1)} collective-permute-done((bf16[8,48,768]{2,1,0:T(8,128)(2,1)S(1)}, bf16[8,48,768]{2,1,0:T(8,128)(2,1)}, u32[]{:S(2)}, u32[]{:S(2)}) %collective-permute-start.21) | collective-permute-done | bytes 589856 | tf_op jit(solution)/shard_map/ppermute | solution.py:68
  104.8 10.2 %feed0.1 = (bf16[1,2,4,48,768]{4,3,2,1,0:T(8,128)(2,1)}, bf16[1,2,4,48,768]{4,3,2,1,0:T(8,128)(2,1)}, bf16[2,8,48,768]{3,2,1,0:T(8,128)(2,1)}, f32[1,768]{1,0:T(...) custom-call(s32[16]{0:T(128)} %fusion.16.refs_0_, s32[16]{0:T(128)} %pad_add_fusion.1.refs_1_, ...), custom_call_target="tpu_custom_call" | custom-call | flops 1100000000 | bytes 3500000 | tf_op jit(solution)/shard_map/feed0/pallas_call | solution.py:497
  121.0 10.1 %feed1.1 = (bf16[1,2,4,48,768]{4,3,2,1,0:T(8,128)(2,1)}, bf16[1,2,4,48,768]{4,3,2,1,0:T(8,128)(2,1)}, bf16[2,8,48,768]{3,2,1,0:T(8,128)(2,1)}, f32[1,768]{1,0:T(...) custom-call(s32[16]{0:T(128)} %fusion.16.refs_0_, ...), custom_call_target="tpu_custom_call" | custom-call | flops 1100000000 | bytes 3500000 | tf_op jit(solution)/shard_map/feed1/pallas_call | solution.py:497
  142.5 11.2 %attend_back.1 = (bf16[3,48,768]{2,1,0:T(8,128)(2,1)}, bf16[3,48,768]{2,1,0:T(8,128)(2,1)}, f32[3,96,768]{2,1,0:T(8,128)}, bf16[3,96,768]{2,1,0:T(8,128)(2,1)}, ...) custom-call(s32[16]{0:T(128)} %fusion.16.refs_0_, ...), custom_call_target="tpu_custom_call" | custom-call | flops 1100000000 | bytes 3500000 | tf_op jit(solution)/shard_map/attend_back/pallas_call | solution.py:497
  161.0 7.8 %weights_back.1 = (bf16[2,8,48,768]{3,2,1,0:T(8,128)(2,1)}, bf16[2,8,48,768]{3,2,1,0:T(8,128)(2,1)}, bf16[2,8,48,768]{3,2,1,0:T(8,128)(2,1)}, bf16[2,8,48,768]{3,2,1,0:T(8,128)(2,1)}) custom-call(s32[16]{0:T(128)} %copy-done.73, bf16[288,768]{1,0:T(8,128)(2,1)} %bitcast.280, bf16[288,768]{1,0:T(8,128)(2,1)} %bitcast.282, bf16[624,768]{1,0:T(8,128)(2,1)} %bitcast.264, ...), custom_call_target="tpu_custom_call" | custom-call | flops 1100000000 | bytes 3500000 | tf_op jit(solution)/shard_map/weights_back/pallas_call | solution.py:497
  174.9 10.0 %input_back.1 = (f32[3,48,768]{2,1,0:T(8,128)}, f32[3,50,768]{2,1,0:T(8,128)}, bf16[3,146,768]{2,1,0:T(8,128)(2,1)}, f32[8,768]{1,0:T(8,128)}) custom-call(s32[16]{0:T(128)} %fusion.16.refs_0_, bf16[3,96,768]{2,1,0:T(8,128)(2,1)} %get-tuple-element.522.refs_1_, bf16[3,208,768]{2,1,0:T(8,128)(2,1)} %get-tuple-element.523.refs_2_, ...), custom_call_target="tpu_custom_call" | custom-call | flops 1100000000 | bytes 3500000 | tf_op jit(solution)/shard_map/input_back/pallas_call | solution.py:497
  191.0 3.7 %collective-permute-start.43 = (bf16[96,768]{1,0:T(8,128)(2,1)S(1)}, bf16[96,768]{1,0:T(8,128)(2,1)S(1)}, u32[]{:S(2)}, u32[]{:S(2)}) collective-permute-start(bf16[96,768]{1,0:T(8,128)(2,1)S(1)} %pad_maximum_fusion.23), channel_id=1, source_target_pairs={{0,8},{8,16},{16,24},{24,0},{1,9},{9,17},{17,25},{25,1},{2,10},{10... | collective-permute-start | bytes 442376 | tf_op jit(solution)/shard_map/ppermute | solution.py:56
  197.2 3.5 %collective-permute-done.43 = bf16[96,768]{1,0:T(8,128)(2,1)S(1)} collective-permute-done((bf16[96,768]{1,0:T(8,128)(2,1)S(1)}, bf16[96,768]{1,0:T(8,128)(2,1)S(1)}, u32[]{:S(2)}, u32[]{:S(2)}) %collective-permute-start.43) | collective-permute-done | bytes 147488 | tf_op jit(solution)/shard_map/ppermute | solution.py:56
  201.6 5.2 %collective-permute-done.44 = bf16[96,768]{1,0:T(8,128)(2,1)S(1)} collective-permute-done((bf16[96,768]{1,0:T(8,128)(2,1)S(1)}, bf16[96,768]{1,0:T(8,128)(2,1)S(1)}, u32[]{:S(2)}, u32[]{:S(2)}) %collective-permute-start.44) | collective-permute-done | bytes 147488 | tf_op jit(solution)/shard_map/ppermute | solution.py:56
  209.5 3.7 %collective-permute-start.51 = (bf16[96,768]{1,0:T(8,128)(2,1)S(1)}, bf16[96,768]{1,0:T(8,128)(2,1)S(1)}, u32[]{:S(2)}, u32[]{:S(2)}) collective-permute-start(bf16[96,768]{1,0:T(8,128)(2,1)S(1)} %pad_maximum_fusion.26), channel_id=1, source_target_pairs={{0,8},{8,16},{16,24},{24,0},{1,9},{9,17},{17,25},{25,1},{2,10},{10... | collective-permute-start | bytes 442376 | tf_op jit(solution)/shard_map/ppermute | solution.py:56
  219.4 4.4 %collective-permute-done.52 = bf16[96,768]{1,0:T(8,128)(2,1)S(1)} collective-permute-done((bf16[96,768]{1,0:T(8,128)(2,1)S(1)}, bf16[96,768]{1,0:T(8,128)(2,1)S(1)}, u32[]{:S(2)}, u32[]{:S(2)}) %collective-permute-start.52) | collective-permute-done | bytes 147488 | tf_op jit(solution)/shard_map/ppermute | solution.py:56
  224.1 3.9 %collective-permute-start.54 = (bf16[120,768]{1,0:T(8,128)(2,1)S(1)}, bf16[120,768]{1,0:T(8,128)(2,1)S(1)}, u32[]{:S(2)}, u32[]{:S(2)}) collective-permute-start(bf16[120,768]{1,0:T(8,128)(2,1)S(1)} %get-tuple-element.595), channel_id=1, source_target_pairs={{0,8},{8,16},{16,24},{24,0},{1,9},{9,17},{17,25},{25,1},{2,10},{10... | collective-permute-start | bytes 552968 | tf_op jit(solution)/shard_map/ppermute | solution.py:56
  236.7 5.1 %collective-permute-done.55 = bf16[120,768]{1,0:T(8,128)(2,1)S(1)} collective-permute-done((bf16[120,768]{1,0:T(8,128)(2,1)S(1)}, bf16[120,768]{1,0:T(8,128)(2,1)S(1)}, u32[]{:S(2)}, u32[]{:S(2)}) %collective-permute-start.55) | collective-permute-done | bytes 184352 | tf_op jit(solution)/shard_map/ppermute | solution.py:56
  243.9 3.9 %collective-permute-done.50 = bf16[3,146,768]{2,1,0:T(8,128)(2,1)S(1)} collective-permute-done((bf16[3,146,768]{2,1,0:T(8,128)(2,1)}, bf16[3,146,768]{2,1,0:T(8,128)(2,1)S(1)}, u32[]{:S(2)}, u32[]{:S(2)}) %collective-permute-start.50) | collective-permute-done | bytes 672800 | tf_op jit(solution)/shard_map/ppermute | solution.py:68
  (423 shorter events, 106.3 us)
Async XLA Ops:
  6.2 19.2 %collective-permute-start.3 = (bf16[3,146,768]{2,1,0:T(8,128)(2,1)S(1)}, bf16[3,146,768]{2,1,0:T(8,128)(2,1)S(1)}, u32[]{:S(2)}, u32[]{:S(2)}) collective-permute-start(bf16[3,146,768]{2,1,0:T(8,128)(2,1)S(1)} %pad_maximum_fusion.3), channel_id=1, source_target_pairs={{0,1},{1,0},{2,3},{3,2},{4,5},{5,4},{6,7},{7,6},{8,9},{9,8},{10,11... | collective-permute-start | bytes 2018312 | tf_op jit(solution)/shard_map/ppermute | solution.py:68
  10.4 15.0 %collective-permute-start.1 = (bf16[120,768]{1,0:T(8,128)(2,1)S(1)}, bf16[120,768]{1,0:T(8,128)(2,1)S(1)}, u32[]{:S(2)}, u32[]{:S(2)}) collective-permute-start(bf16[120,768]{1,0:T(8,128)(2,1)S(1)} %pack.3), channel_id=1, source_target_pairs={{0,16},{8,24},{16,0},{24,8},{1,17},{9,25},{17,1},{25,9},{2,18},{10... | collective-permute-start | bytes 552968 | tf_op jit(solution)/shard_map/ppermute | solution.py:56
  25.6 16.9 %collective-permute-start.5 = (bf16[216,768]{1,0:T(8,128)(2,1)S(1)}, bf16[216,768]{1,0:T(8,128)(2,1)S(1)}, u32[]{:S(2)}, u32[]{:S(2)}) collective-permute-start(bf16[216,768]{1,0:T(8,128)(2,1)S(1)} %add_dynamic-update-slice_fusion), channel_id=1, source_target_pairs={{0,4},{4,0},{1,5},{5,1},{2,6},{6,2},{3,7},{7,3},{8,12},{12,8},{9,1... | collective-permute-start | bytes 995336 | tf_op jit(solution)/shard_map/ppermute | solution.py:62
  27.1 15.3 %collective-permute-start.6 = (bf16[4,48,768]{2,1,0:T(8,128)(2,1)S(1)}, bf16[4,48,768]{2,1,0:T(8,128)(2,1)S(1)}, u32[]{:S(2)}, u32[]{:S(2)}) collective-permute-start(bf16[4,48,768]{2,1,0:T(8,128)(2,1)S(1)} %pad_maximum_fusion.14), channel_id=1, source_target_pairs={{0,1},{1,0},{2,3},{3,2},{4,5},{5,4},{6,7},{7,6},{8,9},{9,8},{10,11... | collective-permute-start | bytes 884744 | tf_op jit(solution)/shard_map/ppermute | solution.py:68
  44.4 16.5 %collective-permute-start.10 = (bf16[408,768]{1,0:T(8,128)(2,1)S(1)}, bf16[408,768]{1,0:T(8,128)(2,1)S(1)}, u32[]{:S(2)}, u32[]{:S(2)}) collective-permute-start(bf16[408,768]{1,0:T(8,128)(2,1)S(1)} %pad_maximum_fusion.4), channel_id=1, source_target_pairs={{0,1},{1,0},{2,3},{3,2},{4,5},{5,4},{6,7},{7,6},{8,9},{9,8},{10,11... | collective-permute-start | bytes 1880072 | tf_op jit(solution)/shard_map/ppermute | solution.py:68
  46.0 14.9 %collective-permute-start.11 = (bf16[4,2,48,768]{3,2,1,0:T(8,128)(2,1)S(1)}, bf16[4,2,48,768]{3,2,1,0:T(8,128)(2,1)S(1)}, u32[]{:S(2)}, u32[]{:S(2)}) collective-permute-start(bf16[4,2,48,768]{3,2,1,0:T(8,128)(2,1)S(1)} %bitcast.220), channel_id=1, source_target_pairs={{0,4},{4,0},{1,5},{5,1},{2,6},{6,2},{3,7},{7,3},{8,12},{12,8},{9,1... | collective-permute-start | bytes 1769480 | tf_op jit(solution)/shard_map/ppermute | solution.py:62
  63.3 19.0 %collective-permute-start.15 = (bf16[4,96,768]{2,1,0:T(8,128)(2,1)S(1)}, bf16[4,96,768]{2,1,0:T(8,128)(2,1)S(1)}, u32[]{:S(2)}, u32[]{:S(2)}) collective-permute-start(bf16[4,96,768]{2,1,0:T(8,128)(2,1)S(1)} %pad_maximum_fusion.6), channel_id=1, source_target_pairs={{0,4},{4,0},{1,5},{5,1},{2,6},{6,2},{3,7},{7,3},{8,12},{12,8},{9,1... | collective-permute-start | bytes 1769480 | tf_op jit(solution)/shard_map/ppermute | solution.py:62
  65.1 17.1 %collective-permute-start.16 = (bf16[4,96,768]{2,1,0:T(8,128)(2,1)S(1)}, bf16[4,96,768]{2,1,0:T(8,128)(2,1)S(1)}, u32[]{:S(2)}, u32[]{:S(2)}) collective-permute-start(bf16[4,96,768]{2,1,0:T(8,128)(2,1)S(1)} %pad_maximum_fusion.7), channel_id=1, source_target_pairs={{0,1},{1,0},{2,3},{3,2},{4,5},{5,4},{6,7},{7,6},{8,9},{9,8},{10,11... | collective-permute-start | bytes 1769480 | tf_op jit(solution)/shard_map/ppermute | solution.py:68
  85.4 16.5 %collective-permute-start.25 = (bf16[3,146,768]{2,1,0:T(8,128)(2,1)S(1)}, bf16[3,146,768]{2,1,0:T(8,128)(2,1)S(1)}, u32[]{:S(2)}, u32[]{:S(2)}) collective-permute-start(bf16[3,146,768]{2,1,0:T(8,128)(2,1)S(1)} %copy-done.19), channel_id=1, source_target_pairs={{0,2},{2,0},{1,3},{3,1},{4,6},{6,4},{5,7},{7,5},{8,10},{10,8},{9,1... | collective-permute-start | bytes 2018312 | tf_op jit(solution)/shard_map/ppermute | solution.py:65
  85.4 15.8 %collective-permute-start.21 = (bf16[8,48,768]{2,1,0:T(8,128)(2,1)S(1)}, bf16[8,48,768]{2,1,0:T(8,128)(2,1)}, u32[]{:S(2)}, u32[]{:S(2)}) collective-permute-start(bf16[8,48,768]{2,1,0:T(8,128)(2,1)S(1)} %pad_maximum_fusion.8), channel_id=1, source_target_pairs={{0,1},{1,0},{2,3},{3,2},{4,5},{5,4},{6,7},{7,6},{8,9},{9,8},{10,11... | collective-permute-start | bytes 1769480 | tf_op jit(solution)/shard_map/ppermute | solution.py:68
  86.4 15.6 %collective-permute-start.22 = (bf16[4,2,48,768]{3,2,1,0:T(8,128)(2,1)S(1)}, bf16[4,2,48,768]{3,2,1,0:T(8,128)(2,1)}, u32[]{:S(2)}, u32[]{:S(2)}) collective-permute-start(bf16[4,2,48,768]{3,2,1,0:T(8,128)(2,1)S(1)} %bitcast.240), channel_id=1, source_target_pairs={{0,4},{4,0},{1,5},{5,1},{2,6},{6,2},{3,7},{7,3},{8,12},{12,8},{9,1... | collective-permute-start | bytes 1769480 | tf_op jit(solution)/shard_map/ppermute | solution.py:62
  102.0 14.6 %collective-permute-start.26 = (bf16[8,48,768]{2,1,0:T(8,128)(2,1)S(1)}, bf16[8,48,768]{2,1,0:T(8,128)(2,1)S(1)}, u32[]{:S(2)}, u32[]{:S(2)}) collective-permute-start(bf16[8,48,768]{2,1,0:T(8,128)(2,1)S(1)} %pad_maximum_fusion.10), channel_id=1, source_target_pairs={{0,1},{1,0},{2,3},{3,2},{4,5},{5,4},{6,7},{7,6},{8,9},{9,8},{10,11... | collective-permute-start | bytes 1769480 | tf_op jit(solution)/shard_map/ppermute | solution.py:68
  103.0 14.4 %collective-permute-start.27 = (bf16[4,2,48,768]{3,2,1,0:T(8,128)(2,1)S(1)}, bf16[4,2,48,768]{3,2,1,0:T(8,128)(2,1)S(1)}, u32[]{:S(2)}, u32[]{:S(2)}) collective-permute-start(bf16[4,2,48,768]{3,2,1,0:T(8,128)(2,1)S(1)} %bitcast.243), channel_id=1, source_target_pairs={{0,4},{4,0},{1,5},{5,1},{2,6},{6,2},{3,7},{7,3},{8,12},{12,8},{9,1... | collective-permute-start | bytes 1769480 | tf_op jit(solution)/shard_map/ppermute | solution.py:62
  118.7 16.3 %collective-permute-start.30 = (bf16[576,768]{1,0:T(8,128)(2,1)S(1)}, bf16[576,768]{1,0:T(8,128)(2,1)S(1)}, u32[]{:S(2)}, u32[]{:S(2)}) collective-permute-start(bf16[576,768]{1,0:T(8,128)(2,1)S(1)} %copy-done.77), channel_id=1, source_target_pairs={{0,2},{2,0},{1,3},{3,1},{4,6},{6,4},{5,7},{7,5},{8,10},{10,8},{9,1... | collective-permute-start | bytes 2654216 | tf_op jit(solution)/shard_map/ppermute | solution.py:65
  118.8 16.0 %collective-permute-start.28 = (bf16[1,4,2,48,768]{4,3,1,2,0:T(8,128)(2,1)}, bf16[1,4,2,48,768]{4,3,1,2,0:T(8,128)(2,1)S(1)}, u32[]{:S(2)}, u32[]{:S(2)}) collective-permute-start(bf16[1,4,2,48,768]{4,3,1,2,0:T(8,128)(2,1)} %bitcast.298), channel_id=1, source_target_pairs={{0,4},{4,0},{1,5},{5,1},{2,6},{6,2},{3,7},{7,3},{8,12},{12,8},{9,1... | collective-permute-start | bytes 1769480 | tf_op jit(solution)/shard_map/ppermute | solution.py:62
  119.6 15.4 %collective-permute-start.29 = (bf16[2,8,24,768]{3,2,0,1:T(8,128)(2,1)S(1)}, bf16[2,8,24,768]{3,2,0,1:T(8,128)(2,1)S(1)}, u32[]{:S(2)}, u32[]{:S(2)}) collective-permute-start(bf16[2,8,24,768]{3,2,0,1:T(8,128)(2,1)S(1)} %copy_bitcast_fusion), channel_id=1, source_target_pairs={{0,1},{1,0},{2,3},{3,2},{4,5},{5,4},{6,7},{7,6},{8,9},{9,8},{10,11... | collective-permute-start | bytes 1769480 | tf_op jit(solution)/shard_map/ppermute | solution.py:68
  137.8 16.1 %collective-permute-start.33 = (bf16[1,4,2,48,768]{4,3,1,2,0:T(8,128)(2,1)}, bf16[1,4,2,48,768]{4,3,1,2,0:T(8,128)(2,1)}, u32[]{:S(2)}, u32[]{:S(2)}) collective-permute-start(bf16[1,4,2,48,768]{4,3,1,2,0:T(8,128)(2,1)} %bitcast.297), channel_id=1, source_target_pairs={{0,4},{4,0},{1,5},{5,1},{2,6},{6,2},{3,7},{7,3},{8,12},{12,8},{9,1... | collective-permute-start | bytes 1769480 | tf_op jit(solution)/shard_map/ppermute | solution.py:62
  139.0 14.9 %collective-permute-start.34 = (bf16[2,8,24,768]{3,2,1,0:T(8,128)(2,1)}, bf16[2,8,24,768]{3,2,1,0:T(8,128)(2,1)}, u32[]{:S(2)}, u32[]{:S(2)}) collective-permute-start(bf16[2,8,24,768]{3,2,1,0:T(8,128)(2,1)} %dynamic-slice_bitcast_fusion), channel_id=1, source_target_pairs={{0,1},{1,0},{2,3},{3,2},{4,5},{5,4},{6,7},{7,6},{8,9},{9,8},{10,11... | collective-permute-start | bytes 1769480 | tf_op jit(solution)/shard_map/ppermute | solution.py:68
  156.0 12.8 %collective-permute-start.35 = (bf16[1,4,48,768]{3,2,1,0:T(8,128)(2,1)S(1)}, bf16[1,4,48,768]{3,2,1,0:T(8,128)(2,1)S(1)}, u32[]{:S(2)}, u32[]{:S(2)}) collective-permute-start(bf16[1,4,48,768]{3,2,1,0:T(8,128)(2,1)S(1)} %fusion.8), channel_id=1, source_target_pairs={{0,1},{1,0},{2,3},{3,2},{4,5},{5,4},{6,7},{7,6},{8,9},{9,8},{10,11... | collective-permute-start | bytes 884744 | tf_op jit(solution)/shard_map/ppermute | solution.py:68
  173.3 12.8 %collective-permute-start.39 = (bf16[2,8,2,24,768]{4,3,0,1,2:T(8,128)(2,1)S(1)}, bf16[2,8,2,24,768]{4,3,0,1,2:T(8,128)(2,1)S(1)}, u32[]{:S(2)}, u32[]{:S(2)}) collective-permute-start(bf16[2,8,2,24,768]{4,3,0,1,2:T(8,128)(2,1)S(1)} %copy.127), channel_id=1, source_target_pairs={{0,2},{2,0},{1,3},{3,1},{4,6},{6,4},{5,7},{7,5},{8,10},{10,8},{9,1... | collective-permute-start | bytes 3538952 | tf_op jit(solution)/shard_map/ppermute | solution.py:65
  188.7 18.2 %collective-permute-start.41 = (bf16[2,4,2,24,768]{4,3,0,1,2:T(8,128)(2,1)S(1)}, bf16[2,4,2,24,768]{4,3,0,1,2:T(8,128)(2,1)S(1)}, u32[]{:S(2)}, u32[]{:S(2)}) collective-permute-start(bf16[2,4,2,24,768]{4,3,0,1,2:T(8,128)(2,1)S(1)} %add_convert_fusion.1), channel_id=1, source_target_pairs={{0,4},{4,0},{1,5},{5,1},{2,6},{6,2},{3,7},{7,3},{8,12},{12,8},{9,1... | collective-permute-start | bytes 1769480 | tf_op jit(solution)/shard_map/ppermute | solution.py:62
  189.9 17.0 %collective-permute-start.42 = (bf16[2,8,24,768]{3,2,0,1:T(8,128)(2,1)S(1)}, bf16[2,8,24,768]{3,2,0,1:T(8,128)(2,1)S(1)}, u32[]{:S(2)}, u32[]{:S(2)}) collective-permute-start(bf16[2,8,24,768]{3,2,0,1:T(8,128)(2,1)S(1)} %fusion.1), channel_id=1, source_target_pairs={{0,1},{1,0},{2,3},{3,2},{4,5},{5,4},{6,7},{7,6},{8,9},{9,8},{10,11... | collective-permute-start | bytes 1769480 | tf_op jit(solution)/shard_map/ppermute | solution.py:68
  228.0 13.8 %collective-permute-start.55 = (bf16[120,768]{1,0:T(8,128)(2,1)S(1)}, bf16[120,768]{1,0:T(8,128)(2,1)S(1)}, u32[]{:S(2)}, u32[]{:S(2)}) collective-permute-start(bf16[120,768]{1,0:T(8,128)(2,1)S(1)} %get-tuple-element.596), channel_id=1, source_target_pairs={{0,16},{8,24},{16,0},{24,8},{1,17},{9,25},{17,1},{25,9},{2,18},{10... | collective-permute-start | bytes 552968 | tf_op jit(solution)/shard_map/ppermute | solution.py:56
  230.5 17.3 %collective-permute-start.50 = (bf16[3,146,768]{2,1,0:T(8,128)(2,1)}, bf16[3,146,768]{2,1,0:T(8,128)(2,1)S(1)}, u32[]{:S(2)}, u32[]{:S(2)}) collective-permute-start(bf16[3,146,768]{2,1,0:T(8,128)(2,1)} %get-tuple-element.576), channel_id=1, source_target_pairs={{0,1},{1,0},{2,3},{3,2},{4,5},{5,4},{6,7},{7,6},{8,9},{9,8},{10,11... | collective-permute-start | bytes 2018312 | tf_op jit(solution)/shard_map/ppermute | solution.py:68
  (115 other events, 740.9 us)

commit v2 on v1

--- a/solution.py
+++ b/solution.py
@@ -483,7 +483,7 @@
         finish(wholes[index], sems.at[index])
 
 
-def call(name, kernel, grid, ins, outs, operands, scratch=(), after=(), us=1, mib=54):
+def call(name, kernel, grid, ins, outs, operands, scratch=(), after=(), us=3, mib=54):
     ins = list(ins) + [ANY] * len(after)
     operands = tuple(operands) + tuple(after)
 

time: 252 us -> 250 us (level)
  local copies, waits for them, and re-layouts: 30.2 us -> 25.9 us
  waiting for transfers between devices: 66.1 us -> 68.7 us
    unnamed x156 -> x128, local copies, waits for them, and re-layouts: 12.2 us -> 9.25 us
  transfers between devices with their start and end apart: 58 -> 58, of which waited for: 25 -> 24; matrix products, arithmetic and copies ran while one was open for 7% -> 8% of each run, Pallas kernels for 26% -> 27%
where the time goes in v2:
time: 250 us; the launch traced here: 249 us
  waiting for transfers between devices  68.7 us (27%)
  starting transfers between devices  67.1 us (27%)
  Pallas kernels  66.4 us (27%)
  local copies, waits for them, and re-layouts  25.9 us (10%)
  other arithmetic  18.5 us (7%)
  between operations  2.54 us (1%)
    pallas_call x10, Pallas kernels, call(): pl.pallas_call(kernel, name=name, grid=grid, in_specs=[spec(pltpu.HBM if...  66.4 us
    ppermute x18, waiting for transfers between devices, turn(): lax.ppermute(values, 'ring', [(place, (place + step) % self.ring) for pla...  39.2 us
    ppermute x18, starting transfers between devices, turn(): lax.ppermute(values, 'ring', [(place, (place + step) % self.ring) for pla...  36 us
    ppermute x14, waiting for transfers between devices, swap_y(): return lax.ppermute(values, 'query', [(0, 1), (1, 0)])  19.8 us
    ppermute x14, starting transfers between devices, swap_y(): return lax.ppermute(values, 'query', [(0, 1), (1, 0)])  17.5 us
    ppermute x11, starting transfers between devices, swap_x(): return lax.ppermute(values, 'x', [(0, 1), (1, 0)])  10.6 us
    unnamed x128, local copies, waits for them, and re-layouts  9.25 us
    ppermute x11, waiting for transfers between devices, swap_x(): return lax.ppermute(values, 'x', [(0, 1), (1, 0)])  5.71 us
  transfers between devices with their start and end apart: 58, of which 24 were waited for; matrix products, arithmetic and copies ran while one was open for 8% of the time, Pallas kernels for 27%

profile of v2, /device:TPU:0, one launch (start us, length us, event | category | flops | bytes accessed | tf_op | source)
XLA Modules:
  0.0 249.0 jit_solution(4334248322980718160)
XLA Ops:
  6.2 2.6 %collective-permute-start.3 = (bf16[3,146,768]{2,1,0:T(8,128)(2,1)S(1)}, bf16[3,146,768]{2,1,0:T(8,128)(2,1)S(1)}, u32[]{:S(2)}, u32[]{:S(2)}) collective-permute-start(bf16[3,146,768]{2,1,0:T(8,128)(2,1)S(1)} %pad_maximum_fusion.3), channel_id=1, source_target_pairs={{0,1},{1,0},{2,3},{3,2},{4,5},{5,4},{6,7},{7,6},{8,9},{9,8},{10,11... | collective-permute-start | bytes 2018312 | tf_op jit(solution)/shard_map/ppermute | solution.py:68
  14.8 3.4 %collective-permute-done = bf16[120,768]{1,0:T(8,128)(2,1)S(1)} collective-permute-done((bf16[120,768]{1,0:T(8,128)(2,1)S(1)}, bf16[120,768]{1,0:T(8,128)(2,1)S(1)}, u32[]{:S(2)}, u32[]{:S(2)}) %collective-permute-start) | collective-permute-done | bytes 184352 | tf_op jit(solution)/shard_map/ppermute | solution.py:56
  18.2 7.2 %collective-permute-done.1 = bf16[120,768]{1,0:T(8,128)(2,1)S(1)} collective-permute-done((bf16[120,768]{1,0:T(8,128)(2,1)S(1)}, bf16[120,768]{1,0:T(8,128)(2,1)S(1)}, u32[]{:S(2)}, u32[]{:S(2)}) %collective-permute-start.1) | collective-permute-done | bytes 184352 | tf_op jit(solution)/shard_map/ppermute | solution.py:56
  29.5 3.5 %collective-permute-start.7 = (bf16[96,768]{1,0:T(8,128)(2,1)S(1)}, bf16[96,768]{1,0:T(8,128)(2,1)S(1)}, u32[]{:S(2)}, u32[]{:S(2)}) collective-permute-start(bf16[96,768]{1,0:T(8,128)(2,1)S(1)} %pack.4), channel_id=1, source_target_pairs={{0,8},{8,16},{16,24},{24,0},{1,9},{9,17},{17,25},{25,1},{2,10},{10... | collective-permute-start | bytes 442376 | tf_op jit(solution)/shard_map/ppermute | solution.py:56
  35.3 5.1 %prepare.1 = (f32[3,208,768]{2,1,0:T(8,128)}, f32[3,208,768]{2,1,0:T(8,128)}, f32[3,208,1]{2,1,0:T(8,128)}, f32[3,208,1]{2,1,0:T(8,128)}) custom-call(s32[3,208,2]{2,1,0:T(8,128)} %copy.113.place_ref, bf16[3,48,768]{2,1,0:T(8,128)(2,1)} %get-tuple-element.644.own_ref.refs_3_.refs_15_, bf16[3,50,768]{2,1,0:T(8,128)(2,1)} %get-tuple-element.642.own_latent_ref, ...), custom_call_target="tpu_custom_call" | custom-call | flops 3300000000 | bytes 10500000 | tf_op jit(solution)/shard_map/prepare/pallas_call | solution.py:497
  40.5 2.8 %collective-permute-done.8 = bf16[96,768]{1,0:T(8,128)(2,1)S(1)} collective-permute-done((bf16[96,768]{1,0:T(8,128)(2,1)S(1)}, bf16[96,768]{1,0:T(8,128)(2,1)S(1)}, u32[]{:S(2)}, u32[]{:S(2)}) %collective-permute-start.8) | collective-permute-done | bytes 147488 | tf_op jit(solution)/shard_map/ppermute | solution.py:56
  45.7 3.6 %collective-permute-start.12 = (bf16[96,768]{1,0:T(8,128)(2,1)S(1)}, bf16[96,768]{1,0:T(8,128)(2,1)S(1)}, u32[]{:S(2)}, u32[]{:S(2)}) collective-permute-start(bf16[96,768]{1,0:T(8,128)(2,1)S(1)} %pack.5), channel_id=1, source_target_pairs={{0,8},{8,16},{16,24},{24,0},{1,9},{9,17},{17,25},{25,1},{2,10},{10... | collective-permute-start | bytes 442376 | tf_op jit(solution)/shard_map/ppermute | solution.py:56
  51.7 3.6 %collective-permute-done.12 = bf16[96,768]{1,0:T(8,128)(2,1)S(1)} collective-permute-done((bf16[96,768]{1,0:T(8,128)(2,1)S(1)}, bf16[96,768]{1,0:T(8,128)(2,1)S(1)}, u32[]{:S(2)}, u32[]{:S(2)}) %collective-permute-start.12) | collective-permute-done | bytes 147488 | tf_op jit(solution)/shard_map/ppermute | solution.py:56
  55.3 4.4 %collective-permute-done.13 = bf16[96,768]{1,0:T(8,128)(2,1)S(1)} collective-permute-done((bf16[96,768]{1,0:T(8,128)(2,1)S(1)}, bf16[96,768]{1,0:T(8,128)(2,1)S(1)}, u32[]{:S(2)}, u32[]{:S(2)}) %collective-permute-start.13) | collective-permute-done | bytes 147488 | tf_op jit(solution)/shard_map/ppermute | solution.py:56
  69.9 12.0 %attend.1 = (bf16[3,96,768]{2,1,0:T(8,128)(2,1)}, bf16[3,208,768]{2,1,0:T(8,128)(2,1)}, bf16[3,208,768]{2,1,0:T(8,128)(2,1)}, bf16[3,3,208,384]{3,2,1,0:T(8,128)...) custom-call(s32[16]{0:T(128)} %fusion.16.refs_0_, ...), custom_call_target="tpu_custom_call" | custom-call | flops 3300000000 | bytes 10500000 | tf_op jit(solution)/shard_map/attend/pallas_call | solution.py:497
  87.9 11.4 %collective-permute-done.21 = bf16[8,48,768]{2,1,0:T(8,128)(2,1)S(1)} collective-permute-done((bf16[8,48,768]{2,1,0:T(8,128)(2,1)S(1)}, bf16[8,48,768]{2,1,0:T(8,128)(2,1)S(1)}, u32[]{:S(2)}, u32[]{:S(2)}) %collective-permute-start.21) | collective-permute-done | bytes 589856 | tf_op jit(solution)/shard_map/ppermute | solution.py:68
  102.3 10.1 %feed0.1 = (bf16[1,2,4,48,768]{4,3,2,1,0:T(8,128)(2,1)}, bf16[1,2,4,48,768]{4,3,2,1,0:T(8,128)(2,1)}, bf16[2,8,48,768]{3,2,1,0:T(8,128)(2,1)}, f32[1,768]{1,0:T(...) custom-call(s32[16]{0:T(128)} %fusion.16.refs_0_, s32[16]{0:T(128)} %pad_add_fusion.1.refs_1_, ...), custom_call_target="tpu_custom_call" | custom-call | flops 3300000000 | bytes 10500000 | tf_op jit(solution)/shard_map/feed0/pallas_call | solution.py:497
  119.7 10.2 %feed1.1 = (bf16[1,2,4,48,768]{4,3,2,1,0:T(8,128)(2,1)}, bf16[1,2,4,48,768]{4,3,2,1,0:T(8,128)(2,1)}, bf16[2,8,48,768]{3,2,1,0:T(8,128)(2,1)}, f32[1,768]{1,0:T(...) custom-call(s32[16]{0:T(128)} %fusion.16.refs_0_, ...), custom_call_target="tpu_custom_call" | custom-call | flops 3300000000 | bytes 10500000 | tf_op jit(solution)/shard_map/feed1/pallas_call | solution.py:497
  140.8 10.7 %attend_back.1 = (bf16[3,48,768]{2,1,0:T(8,128)(2,1)}, bf16[3,48,768]{2,1,0:T(8,128)(2,1)}, f32[3,96,768]{2,1,0:T(8,128)}, bf16[3,96,768]{2,1,0:T(8,128)(2,1)}, ...) custom-call(s32[16]{0:T(128)} %fusion.16.refs_0_, ...), custom_call_target="tpu_custom_call" | custom-call | flops 3300000000 | bytes 10500000 | tf_op jit(solution)/shard_map/attend_back/pallas_call | solution.py:497
  157.9 8.0 %weights_back.1 = (bf16[2,8,48,768]{3,2,1,0:T(8,128)(2,1)}, bf16[2,8,48,768]{3,2,1,0:T(8,128)(2,1)}, bf16[2,8,48,768]{3,2,1,0:T(8,128)(2,1)}, bf16[2,8,48,768]{3,2,1,0:T(8,128)(2,1)}) custom-call(s32[16]{0:T(128)} %copy-done.57, bf16[288,768]{1,0:T(8,128)(2,1)} %bitcast.294, bf16[288,768]{1,0:T(8,128)(2,1)} %bitcast.291, bf16[624,768]{1,0:T(8,128)(2,1)} %bitcast.293, ...), custom_call_target="tpu_custom_call" | custom-call | flops 3300000000 | bytes 10500000 | tf_op jit(solution)/shard_map/weights_back/pallas_call | solution.py:497
  174.5 10.0 %input_back.1 = (f32[3,48,768]{2,1,0:T(8,128)}, f32[3,50,768]{2,1,0:T(8,128)}, bf16[3,146,768]{2,1,0:T(8,128)(2,1)}, f32[8,768]{1,0:T(8,128)}) custom-call(s32[16]{0:T(128)} %fusion.16.refs_0_, bf16[3,96,768]{2,1,0:T(8,128)(2,1)} %get-tuple-element.522.refs_1_, bf16[3,208,768]{2,1,0:T(8,128)(2,1)} %get-tuple-element.523.refs_2_, ...), custom_call_target="tpu_custom_call" | custom-call | flops 3300000000 | bytes 10500000 | tf_op jit(solution)/shard_map/input_back/pallas_call | solution.py:497
  189.4 3.7 %collective-permute-start.43 = (bf16[96,768]{1,0:T(8,128)(2,1)S(1)}, bf16[96,768]{1,0:T(8,128)(2,1)S(1)}, u32[]{:S(2)}, u32[]{:S(2)}) collective-permute-start(bf16[96,768]{1,0:T(8,128)(2,1)S(1)} %pad_maximum_fusion.23), channel_id=1, source_target_pairs={{0,8},{8,16},{16,24},{24,0},{1,9},{9,17},{17,25},{25,1},{2,10},{10... | collective-permute-start | bytes 442376 | tf_op jit(solution)/shard_map/ppermute | solution.py:56
  195.6 3.6 %collective-permute-done.43 = bf16[96,768]{1,0:T(8,128)(2,1)S(1)} collective-permute-done((bf16[96,768]{1,0:T(8,128)(2,1)S(1)}, bf16[96,768]{1,0:T(8,128)(2,1)S(1)}, u32[]{:S(2)}, u32[]{:S(2)}) %collective-permute-start.43) | collective-permute-done | bytes 147488 | tf_op jit(solution)/shard_map/ppermute | solution.py:56
  200.0 5.2 %collective-permute-done.44 = bf16[96,768]{1,0:T(8,128)(2,1)S(1)} collective-permute-done((bf16[96,768]{1,0:T(8,128)(2,1)S(1)}, bf16[96,768]{1,0:T(8,128)(2,1)S(1)}, u32[]{:S(2)}, u32[]{:S(2)}) %collective-permute-start.44) | collective-permute-done | bytes 147488 | tf_op jit(solution)/shard_map/ppermute | solution.py:56
  207.7 3.8 %collective-permute-start.51 = (bf16[96,768]{1,0:T(8,128)(2,1)S(1)}, bf16[96,768]{1,0:T(8,128)(2,1)S(1)}, u32[]{:S(2)}, u32[]{:S(2)}) collective-permute-start(bf16[96,768]{1,0:T(8,128)(2,1)S(1)} %pad_maximum_fusion.26), channel_id=1, source_target_pairs={{0,8},{8,16},{16,24},{24,0},{1,9},{9,17},{17,25},{25,1},{2,10},{10... | collective-permute-start | bytes 442376 | tf_op jit(solution)/shard_map/ppermute | solution.py:56
  217.8 3.9 %collective-permute-done.52 = bf16[96,768]{1,0:T(8,128)(2,1)S(1)} collective-permute-done((bf16[96,768]{1,0:T(8,128)(2,1)S(1)}, bf16[96,768]{1,0:T(8,128)(2,1)S(1)}, u32[]{:S(2)}, u32[]{:S(2)}) %collective-permute-start.52) | collective-permute-done | bytes 147488 | tf_op jit(solution)/shard_map/ppermute | solution.py:56
  222.1 3.9 %collective-permute-start.54 = (bf16[120,768]{1,0:T(8,128)(2,1)S(1)}, bf16[120,768]{1,0:T(8,128)(2,1)S(1)}, u32[]{:S(2)}, u32[]{:S(2)}) collective-permute-start(bf16[120,768]{1,0:T(8,128)(2,1)S(1)} %get-tuple-element.595), channel_id=1, source_target_pairs={{0,8},{8,16},{16,24},{24,0},{1,9},{9,17},{17,25},{25,1},{2,10},{10... | collective-permute-start | bytes 552968 | tf_op jit(solution)/shard_map/ppermute | solution.py:56
  234.6 5.1 %collective-permute-done.55 = bf16[120,768]{1,0:T(8,128)(2,1)S(1)} collective-permute-done((bf16[120,768]{1,0:T(8,128)(2,1)S(1)}, bf16[120,768]{1,0:T(8,128)(2,1)S(1)}, u32[]{:S(2)}, u32[]{:S(2)}) %collective-permute-start.55) | collective-permute-done | bytes 184352 | tf_op jit(solution)/shard_map/ppermute | solution.py:56
  241.9 3.8 %collective-permute-done.50 = bf16[3,146,768]{2,1,0:T(8,128)(2,1)S(1)} collective-permute-done((bf16[3,146,768]{2,1,0:T(8,128)(2,1)}, bf16[3,146,768]{2,1,0:T(8,128)(2,1)S(1)}, u32[]{:S(2)}, u32[]{:S(2)}) %collective-permute-start.50) | collective-permute-done | bytes 672800 | tf_op jit(solution)/shard_map/ppermute | solution.py:68
  (395 shorter events, 104.9 us)
Async XLA Ops:
  6.2 19.2 %collective-permute-start.3 = (bf16[3,146,768]{2,1,0:T(8,128)(2,1)S(1)}, bf16[3,146,768]{2,1,0:T(8,128)(2,1)S(1)}, u32[]{:S(2)}, u32[]{:S(2)}) collective-permute-start(bf16[3,146,768]{2,1,0:T(8,128)(2,1)S(1)} %pad_maximum_fusion.3), channel_id=1, source_target_pairs={{0,1},{1,0},{2,3},{3,2},{4,5},{5,4},{6,7},{7,6},{8,9},{9,8},{10,11... | collective-permute-start | bytes 2018312 | tf_op jit(solution)/shard_map/ppermute | solution.py:68
  10.4 15.0 %collective-permute-start.1 = (bf16[120,768]{1,0:T(8,128)(2,1)S(1)}, bf16[120,768]{1,0:T(8,128)(2,1)S(1)}, u32[]{:S(2)}, u32[]{:S(2)}) collective-permute-start(bf16[120,768]{1,0:T(8,128)(2,1)S(1)} %pack.3), channel_id=1, source_target_pairs={{0,16},{8,24},{16,0},{24,8},{1,17},{9,25},{17,1},{25,9},{2,18},{10... | collective-permute-start | bytes 552968 | tf_op jit(solution)/shard_map/ppermute | solution.py:56
  25.6 17.8 %collective-permute-start.5 = (bf16[216,768]{1,0:T(8,128)(2,1)S(1)}, bf16[216,768]{1,0:T(8,128)(2,1)S(1)}, u32[]{:S(2)}, u32[]{:S(2)}) collective-permute-start(bf16[216,768]{1,0:T(8,128)(2,1)S(1)} %add_dynamic-update-slice_fusion), channel_id=1, source_target_pairs={{0,4},{4,0},{1,5},{5,1},{2,6},{6,2},{3,7},{7,3},{8,12},{12,8},{9,1... | collective-permute-start | bytes 995336 | tf_op jit(solution)/shard_map/ppermute | solution.py:62
  28.0 15.3 %collective-permute-start.6 = (bf16[4,48,768]{2,1,0:T(8,128)(2,1)S(1)}, bf16[4,48,768]{2,1,0:T(8,128)(2,1)S(1)}, u32[]{:S(2)}, u32[]{:S(2)}) collective-permute-start(bf16[4,48,768]{2,1,0:T(8,128)(2,1)S(1)} %pad_maximum_fusion.14), channel_id=1, source_target_pairs={{0,1},{1,0},{2,3},{3,2},{4,5},{5,4},{6,7},{7,6},{8,9},{9,8},{10,11... | collective-permute-start | bytes 884744 | tf_op jit(solution)/shard_map/ppermute | solution.py:68
  43.6 16.5 %collective-permute-start.10 = (bf16[408,768]{1,0:T(8,128)(2,1)S(1)}, bf16[408,768]{1,0:T(8,128)(2,1)S(1)}, u32[]{:S(2)}, u32[]{:S(2)}) collective-permute-start(bf16[408,768]{1,0:T(8,128)(2,1)S(1)} %pad_maximum_fusion.4), channel_id=1, source_target_pairs={{0,1},{1,0},{2,3},{3,2},{4,5},{5,4},{6,7},{7,6},{8,9},{9,8},{10,11... | collective-permute-start | bytes 1880072 | tf_op jit(solution)/shard_map/ppermute | solution.py:68
  45.1 14.9 %collective-permute-start.11 = (bf16[4,2,48,768]{3,2,1,0:T(8,128)(2,1)S(1)}, bf16[4,2,48,768]{3,2,1,0:T(8,128)(2,1)S(1)}, u32[]{:S(2)}, u32[]{:S(2)}) collective-permute-start(bf16[4,2,48,768]{3,2,1,0:T(8,128)(2,1)S(1)} %bitcast.223), channel_id=1, source_target_pairs={{0,4},{4,0},{1,5},{5,1},{2,6},{6,2},{3,7},{7,3},{8,12},{12,8},{9,1... | collective-permute-start | bytes 1769480 | tf_op jit(solution)/shard_map/ppermute | solution.py:62
  63.0 18.9 %collective-permute-start.15 = (bf16[4,96,768]{2,1,0:T(8,128)(2,1)S(1)}, bf16[4,96,768]{2,1,0:T(8,128)(2,1)S(1)}, u32[]{:S(2)}, u32[]{:S(2)}) collective-permute-start(bf16[4,96,768]{2,1,0:T(8,128)(2,1)S(1)} %pad_maximum_fusion.6), channel_id=1, source_target_pairs={{0,4},{4,0},{1,5},{5,1},{2,6},{6,2},{3,7},{7,3},{8,12},{12,8},{9,1... | collective-permute-start | bytes 1769480 | tf_op jit(solution)/shard_map/ppermute | solution.py:62
  66.0 15.9 %collective-permute-start.16 = (bf16[4,96,768]{2,1,0:T(8,128)(2,1)S(1)}, bf16[4,96,768]{2,1,0:T(8,128)(2,1)S(1)}, u32[]{:S(2)}, u32[]{:S(2)}) collective-permute-start(bf16[4,96,768]{2,1,0:T(8,128)(2,1)S(1)} %pad_maximum_fusion.7), channel_id=1, source_target_pairs={{0,1},{1,0},{2,3},{3,2},{4,5},{5,4},{6,7},{7,6},{8,9},{9,8},{10,11... | collective-permute-start | bytes 1769480 | tf_op jit(solution)/shard_map/ppermute | solution.py:68
  83.5 16.4 %collective-permute-start.25 = (bf16[3,146,768]{2,1,0:T(8,128)(2,1)S(1)}, bf16[3,146,768]{2,1,0:T(8,128)(2,1)}, u32[]{:S(2)}, u32[]{:S(2)}) collective-permute-start(bf16[3,146,768]{2,1,0:T(8,128)(2,1)S(1)} %copy-done.25), channel_id=1, source_target_pairs={{0,2},{2,0},{1,3},{3,1},{4,6},{6,4},{5,7},{7,5},{8,10},{10,8},{9,1... | collective-permute-start | bytes 2018312 | tf_op jit(solution)/shard_map/ppermute | solution.py:65
  83.5 15.7 %collective-permute-start.21 = (bf16[8,48,768]{2,1,0:T(8,128)(2,1)S(1)}, bf16[8,48,768]{2,1,0:T(8,128)(2,1)S(1)}, u32[]{:S(2)}, u32[]{:S(2)}) collective-permute-start(bf16[8,48,768]{2,1,0:T(8,128)(2,1)S(1)} %pad_maximum_fusion.8), channel_id=1, source_target_pairs={{0,1},{1,0},{2,3},{3,2},{4,5},{5,4},{6,7},{7,6},{8,9},{9,8},{10,11... | collective-permute-start | bytes 1769480 | tf_op jit(solution)/shard_map/ppermute | solution.py:68
  84.5 15.5 %collective-permute-start.22 = (bf16[4,2,48,768]{3,2,1,0:T(8,128)(2,1)S(1)}, bf16[4,2,48,768]{3,2,1,0:T(8,128)(2,1)S(1)}, u32[]{:S(2)}, u32[]{:S(2)}) collective-permute-start(bf16[4,2,48,768]{3,2,1,0:T(8,128)(2,1)S(1)} %bitcast.261), channel_id=1, source_target_pairs={{0,4},{4,0},{1,5},{5,1},{2,6},{6,2},{3,7},{7,3},{8,12},{12,8},{9,1... | collective-permute-start | bytes 1769480 | tf_op jit(solution)/shard_map/ppermute | solution.py:62
  100.0 14.6 %collective-permute-start.26 = (bf16[8,48,768]{2,1,0:T(8,128)(2,1)S(1)}, bf16[8,48,768]{2,1,0:T(8,128)(2,1)S(1)}, u32[]{:S(2)}, u32[]{:S(2)}) collective-permute-start(bf16[8,48,768]{2,1,0:T(8,128)(2,1)S(1)} %pad_maximum_fusion.10), channel_id=1, source_target_pairs={{0,1},{1,0},{2,3},{3,2},{4,5},{5,4},{6,7},{7,6},{8,9},{9,8},{10,11... | collective-permute-start | bytes 1769480 | tf_op jit(solution)/shard_map/ppermute | solution.py:68
  101.0 14.4 %collective-permute-start.27 = (bf16[4,2,48,768]{3,2,1,0:T(8,128)(2,1)S(1)}, bf16[4,2,48,768]{3,2,1,0:T(8,128)(2,1)S(1)}, u32[]{:S(2)}, u32[]{:S(2)}) collective-permute-start(bf16[4,2,48,768]{3,2,1,0:T(8,128)(2,1)S(1)} %bitcast.264), channel_id=1, source_target_pairs={{0,4},{4,0},{1,5},{5,1},{2,6},{6,2},{3,7},{7,3},{8,12},{12,8},{9,1... | collective-permute-start | bytes 1769480 | tf_op jit(solution)/shard_map/ppermute | solution.py:62
  117.5 16.6 %collective-permute-start.30 = (bf16[576,768]{1,0:T(8,128)(2,1)}, bf16[576,768]{1,0:T(8,128)(2,1)S(1)}, u32[]{:S(2)}, u32[]{:S(2)}) collective-permute-start(bf16[576,768]{1,0:T(8,128)(2,1)} %get-tuple-element.451), channel_id=1, source_target_pairs={{0,2},{2,0},{1,3},{3,1},{4,6},{6,4},{5,7},{7,5},{8,10},{10,8},{9,1... | collective-permute-start | bytes 2654216 | tf_op jit(solution)/shard_map/ppermute | solution.py:65
  117.5 16.1 %collective-permute-start.28 = (bf16[1,4,2,48,768]{4,3,1,2,0:T(8,128)(2,1)}, bf16[1,4,2,48,768]{4,3,1,2,0:T(8,128)(2,1)}, u32[]{:S(2)}, u32[]{:S(2)}) collective-permute-start(bf16[1,4,2,48,768]{4,3,1,2,0:T(8,128)(2,1)} %bitcast.45), channel_id=1, source_target_pairs={{0,4},{4,0},{1,5},{5,1},{2,6},{6,2},{3,7},{7,3},{8,12},{12,8},{9,1... | collective-permute-start | bytes 1769480 | tf_op jit(solution)/shard_map/ppermute | solution.py:62
  118.3 15.8 %collective-permute-start.29 = (bf16[2,8,24,768]{3,2,0,1:T(8,128)(2,1)}, bf16[2,8,24,768]{3,2,0,1:T(8,128)(2,1)}, u32[]{:S(2)}, u32[]{:S(2)}) collective-permute-start(bf16[2,8,24,768]{3,2,0,1:T(8,128)(2,1)} %copy_bitcast_fusion), channel_id=1, source_target_pairs={{0,1},{1,0},{2,3},{3,2},{4,5},{5,4},{6,7},{7,6},{8,9},{9,8},{10,11... | collective-permute-start | bytes 1769480 | tf_op jit(solution)/shard_map/ppermute | solution.py:68
  135.2 16.3 %collective-permute-start.33 = (bf16[1,4,2,48,768]{4,3,1,2,0:T(8,128)(2,1)}, bf16[1,4,2,48,768]{4,3,1,2,0:T(8,128)(2,1)}, u32[]{:S(2)}, u32[]{:S(2)}) collective-permute-start(bf16[1,4,2,48,768]{4,3,1,2,0:T(8,128)(2,1)} %bitcast.53), channel_id=1, source_target_pairs={{0,4},{4,0},{1,5},{5,1},{2,6},{6,2},{3,7},{7,3},{8,12},{12,8},{9,1... | collective-permute-start | bytes 1769480 | tf_op jit(solution)/shard_map/ppermute | solution.py:62
  136.5 15.0 %collective-permute-start.34 = (bf16[2,8,24,768]{3,2,1,0:T(8,128)(2,1)}, bf16[2,8,24,768]{3,2,1,0:T(8,128)(2,1)}, u32[]{:S(2)}, u32[]{:S(2)}) collective-permute-start(bf16[2,8,24,768]{3,2,1,0:T(8,128)(2,1)} %dynamic-slice_bitcast_fusion), channel_id=1, source_target_pairs={{0,1},{1,0},{2,3},{3,2},{4,5},{5,4},{6,7},{7,6},{8,9},{9,8},{10,11... | collective-permute-start | bytes 1769480 | tf_op jit(solution)/shard_map/ppermute | solution.py:68
  169.7 14.9 %collective-permute-start.39 = (bf16[2,8,2,24,768]{4,3,0,1,2:T(8,128)(2,1)S(1)}, bf16[2,8,2,24,768]{4,3,0,1,2:T(8,128)(2,1)S(1)}, u32[]{:S(2)}, u32[]{:S(2)}) collective-permute-start(bf16[2,8,2,24,768]{4,3,0,1,2:T(8,128)(2,1)S(1)} %copy.127), channel_id=1, source_target_pairs={{0,2},{2,0},{1,3},{3,1},{4,6},{6,4},{5,7},{7,5},{8,10},{10,8},{9,1... | collective-permute-start | bytes 3538952 | tf_op jit(solution)/shard_map/ppermute | solution.py:65
  171.0 13.6 %collective-permute-start.40 = (bf16[2,8,2,24,768]{4,3,0,1,2:T(8,128)(2,1)S(1)}, bf16[2,8,2,24,768]{4,3,0,1,2:T(8,128)(2,1)S(1)}, u32[]{:S(2)}, u32[]{:S(2)}) collective-permute-start(bf16[2,8,2,24,768]{4,3,0,1,2:T(8,128)(2,1)S(1)} %copy.128), channel_id=1, source_target_pairs={{0,2},{2,0},{1,3},{3,1},{4,6},{6,4},{5,7},{7,5},{8,10},{10,8},{9,1... | collective-permute-start | bytes 3538952 | tf_op jit(solution)/shard_map/ppermute | solution.py:65
  187.1 18.2 %collective-permute-start.41 = (bf16[2,4,2,24,768]{4,3,0,1,2:T(8,128)(2,1)S(1)}, bf16[2,4,2,24,768]{4,3,0,1,2:T(8,128)(2,1)S(1)}, u32[]{:S(2)}, u32[]{:S(2)}) collective-permute-start(bf16[2,4,2,24,768]{4,3,0,1,2:T(8,128)(2,1)S(1)} %add_convert_fusion.1), channel_id=1, source_target_pairs={{0,4},{4,0},{1,5},{5,1},{2,6},{6,2},{3,7},{7,3},{8,12},{12,8},{9,1... | collective-permute-start | bytes 1769480 | tf_op jit(solution)/shard_map/ppermute | solution.py:62
  187.9 17.3 %collective-permute-start.42 = (bf16[2,8,24,768]{3,2,0,1:T(8,128)(2,1)S(1)}, bf16[2,8,24,768]{3,2,0,1:T(8,128)(2,1)S(1)}, u32[]{:S(2)}, u32[]{:S(2)}) collective-permute-start(bf16[2,8,24,768]{3,2,0,1:T(8,128)(2,1)S(1)} %fusion.1), channel_id=1, source_target_pairs={{0,1},{1,0},{2,3},{3,2},{4,5},{5,4},{6,7},{7,6},{8,9},{9,8},{10,11... | collective-permute-start | bytes 1769480 | tf_op jit(solution)/shard_map/ppermute | solution.py:68
  226.0 13.8 %collective-permute-start.55 = (bf16[120,768]{1,0:T(8,128)(2,1)S(1)}, bf16[120,768]{1,0:T(8,128)(2,1)S(1)}, u32[]{:S(2)}, u32[]{:S(2)}) collective-permute-start(bf16[120,768]{1,0:T(8,128)(2,1)S(1)} %get-tuple-element.596), channel_id=1, source_target_pairs={{0,16},{8,24},{16,0},{24,8},{1,17},{9,25},{17,1},{25,9},{2,18},{10... | collective-permute-start | bytes 552968 | tf_op jit(solution)/shard_map/ppermute | solution.py:56
  228.4 17.3 %collective-permute-start.50 = (bf16[3,146,768]{2,1,0:T(8,128)(2,1)}, bf16[3,146,768]{2,1,0:T(8,128)(2,1)S(1)}, u32[]{:S(2)}, u32[]{:S(2)}) collective-permute-start(bf16[3,146,768]{2,1,0:T(8,128)(2,1)} %get-tuple-element.576), channel_id=1, source_target_pairs={{0,1},{1,0},{2,3},{3,2},{4,5},{5,4},{6,7},{7,6},{8,9},{9,8},{10,11... | collective-permute-start | bytes 2018312 | tf_op jit(solution)/shard_map/ppermute | solution.py:68
  (101 other events, 691.1 us)
